TPU v7x, 128 devices: a whole 4x4x4 slice. The times are simulated.
128 devices in a mesh: dp: 32 (over x, y, core), pipe: 4 (over z).
Axes of the slice: x: 4, y: 4, z: 4, core: 2. Of those that a mesh axis runs over, the one named last changes fastest.
Arguments:
- student_in: bfloat16 [4096, 8192], P('dp', 'pipe'), may hold values from -6 to 6
- value_weight: bfloat16 [4, 8192, 512], P('pipe'), may hold values from -0.0625 to 0.0625
- folded_out: bfloat16 [4, 512, 8192], P('pipe'), may hold values from -0.25 to 0.25
- norm_gain: bfloat16 [4, 8192], P('pipe'), may hold values from 0.5 to 1.5
- proj: bfloat16 [8192, 16384], P('pipe', 'dp'), may hold values from -0.0625 to 0.0625
- teacher_codes: bfloat16 [4096, 16384], P('dp'), may hold values from -12 to 12
- teacher_scales: bfloat16 [4096], P('dp'), may hold values from 0.5 to 3
- perm: int32 [4096], replicated, may hold values from 0 to 4095, each once
Outputs:
- grad_proj: bfloat16 [8192, 16384], P('pipe', 'dp')
- loss: float32 [], replicated
Inputs may be any that keep to these rules, and one draw needn't show every extreme that they name: perm names every store row exactly once.
All inputs are finite; a program needn't handle non-finite values.
Results may differ from a plain program's by a relative error of at most 0.018.
Values may be sent and summed in bfloat16 or wider, within the bound.
A program may use at most 192 MiB of HBM per device.

v0:
```python
import math

import jax
import jax.numpy as jnp
from jax import lax
from jax.sharding import PartitionSpec as P

MICRO = 4


def from_behind(block, axis, distance):
    devices = range(lax.axis_size(axis))
    route = [(i - distance, i) for i in devices if i - distance in devices]
    return lax.ppermute(block, axis, route)


def from_root(block, axis, owner):
    block = jnp.where(lax.axis_index(axis) == owner, block, jnp.zeros_like(block))
    return lax.psum(block, axis)


def norm_rows(hidden, gain):
    values = hidden.astype(jnp.float32)
    scale = lax.rsqrt(jnp.mean(values * values, axis=-1, keepdims=True) + 1e-05)
    return (values * scale * gain.astype(jnp.float32)).astype(jnp.bfloat16)


def apply_layer(hidden, w_value, w_out, gain):
    normed = norm_rows(hidden, gain)
    values = jnp.dot(normed, w_value, preferred_element_type=jnp.float32).astype(jnp.bfloat16)
    branch = jnp.dot(values, w_out, preferred_element_type=jnp.float32)
    return (hidden.astype(jnp.float32) + branch).astype(jnp.bfloat16)


def shards(
    student_in, value_weight, folded_out, norm_gain, proj, teacher_codes, teacher_scales, perm
):
    sections = lax.axis_size("pipe")
    section = lax.axis_index("pipe")
    n_ranks = lax.axis_size("dp")
    full_in = lax.all_gather(student_in, "pipe", axis=1, tiled=True)
    block_rows = full_in.shape[0] // MICRO
    width = full_in.shape[1]
    w_value = value_weight[0]
    w_out = folded_out[0]
    gain = norm_gain[0]
    received = jnp.zeros((block_rows, width), jnp.bfloat16)
    finals = []
    for tick in range(MICRO + sections - 1):
        first_in = min(tick, MICRO - 1) * block_rows
        entering = full_in[first_in : first_in + block_rows]
        layer_in = jnp.where(section == 0, entering, received)
        layer_out = apply_layer(layer_in, w_value, w_out, gain)
        if tick >= sections - 1:
            finals.append(layer_out)
        if tick < MICRO + sections - 2:
            received = from_behind(layer_out, "pipe", 1)
    final_rows = jnp.concatenate(finals, axis=0)
    everywhere = from_root(final_rows, "pipe", sections - 1)
    share_width = width // sections
    my_features = lax.dynamic_slice_in_dim(everywhere, section * share_width, share_width, 1)
    gathered = lax.all_gather(my_features, "dp", axis=0, tiled=True)
    store_rows = teacher_codes.shape[0]
    scale_tiles = jnp.broadcast_to(teacher_scales[:, None], (store_rows, n_ranks))
    codes_all, scales_all = (
        lax.all_to_all(teacher_codes, "dp", split_axis=1, concat_axis=0, tiled=True),
        lax.all_to_all(scale_tiles, "dp", split_axis=1, concat_axis=0, tiled=True),
    )
    tokens_all = gathered.shape[0]
    total_cols = proj.shape[1] * n_ranks
    inv_root = 1.0 / math.sqrt(tokens_all)
    partial_out = jnp.dot(gathered, proj, preferred_element_type=jnp.float32)
    output = lax.psum(partial_out, "pipe")
    target = codes_all[perm].astype(jnp.float32) * scales_all[perm].astype(jnp.float32)
    diff = output - target
    total = lax.psum(jnp.sum(diff * diff), "dp")
    grad_rows = (diff * inv_root).astype(jnp.bfloat16)
    grad_proj = lax.dot_general(
        gathered, grad_rows, (((0,), (0,)), ((), ())), preferred_element_type=jnp.float32
    )
    loss = 0.5 * total / (tokens_all * total_cols)
    return (grad_proj.astype(jnp.bfloat16), loss)


def solution(mesh):
    return jax.shard_map(
        shards,
        mesh=mesh,
        in_specs=(
            P("dp", "pipe"),
            P("pipe", None, None),
            P("pipe", None, None),
            P("pipe", None),
            P("pipe", "dp"),
            P("dp", None),
            P("dp"),
            P(),
        ),
        out_specs=(P("pipe", "dp"), P()),
        check_vma=False,
    )
```

profile of v0, /device:TPU:1, one launch (start us, length us, event | category | flops | bytes accessed | tf_op | source)
XLA Modules:
  0.0 611.8 jit_solution(2712948793176717792)
XLA Ops:
  7.2 0.7 all-gather.3.cloned.1.call-update
  8.0 0.8 mul.183
  8.8 35.2 %all-gather.3.cloned.1.call-done = bf16[128,8192]{1,0:T(8,128)(2,1)} async-done(((bf16[128,2048]{1,0:T(8,128)(2,1)}), bf16[128,8192]{1,0:T(8,128)(2,1)}) %all-gather.3.cloned.1.call-update) | async-done | bytes 2097168 | tf_op jit(solution)/shard_map/all_gather | solution.py:41
  44.0 1.3 fusion.53
  45.3 9.1 %fusion = bf16[32,8192]{1,0:T(8,128)(2,1)S(1)} fusion(bf16[1,512,8192]{2,1,0:T(8,128)(2,1)} %param.10, bf16[1,8192,512]{2,1,0:T(8,128)(2,1)} %param.9, f32[8192]{0:T(1024)S(1)} %bitcast.77, f32[32]{0:T(128)S(1)} %add_rsqrt_fusion.6, bf16[128,8192]{1,0:T(8,128)(2,1)} %all-gather.3.cloned.1.call-done, pred[]{:T(512)S(6)} %eq.5), kind=kOutput, calls=%fused_computation.9 | convolution fusion | flops 539246592 | bytes 18384000 | tf_op jit(solution)/shard_map/dot_general | solution.py:31
  54.4 2.1 collective-permute-start
  56.5 10.5 %collective-permute-done = bf16[32,8192]{1,0:T(8,128)(2,1)S(1)} collective-permute-done((bf16[32,8192]{1,0:T(8,128)(2,1)S(1)}, bf16[32,8192]{1,0:T(8,128)(2,1)S(1)}, u32[]{:S(2)}, u32[]{:S(2)}) %collective-permute-start) | collective-permute-done | bytes 524320 | tf_op jit(solution)/shard_map/ppermute | solution.py:14
  67.0 1.3 fusion.56
  68.4 9.1 %fusion.1 = bf16[32,8192]{1,0:T(8,128)(2,1)S(1)} fusion(bf16[1,512,8192]{2,1,0:T(8,128)(2,1)} %param.10, bf16[1,8192,512]{2,1,0:T(8,128)(2,1)} %param.9, f32[32]{0:T(128)S(1)} %add_rsqrt_fusion.5, f32[8192]{0:T(1024)S(1)} %bitcast.78, bf16[32,8192]{1,0:T(8,128)(2,1)S(1)} %collective-permute-done, bf16[128,8192]{1,0:T(8,128)(2,1)} %all-gather.3.cloned.1.call-done, ...), kind=kOutput, calls=%fused_computation.10 | convolution fusion | flops 539246592 | bytes 19432960 | tf_op jit(solution)/shard_map/dot_general | solution.py:31
  77.5 4.1 collective-permute-start.1
  81.6 9.6 %collective-permute-done.1 = bf16[32,8192]{1,0:T(8,128)(2,1)S(1)} collective-permute-done((bf16[32,8192]{1,0:T(8,128)(2,1)S(1)}, bf16[32,8192]{1,0:T(8,128)(2,1)S(1)}, u32[]{:S(2)}, u32[]{:S(2)}) %collective-permute-start.1) | collective-permute-done | bytes 524320 | tf_op jit(solution)/shard_map/ppermute | solution.py:14
  91.2 1.3 fusion.59
  92.5 9.9 %fusion.2 = bf16[32,8192]{1,0:T(8,128)(2,1)} fusion(bf16[1,512,8192]{2,1,0:T(8,128)(2,1)} %param.10, bf16[1,8192,512]{2,1,0:T(8,128)(2,1)} %param.9, f32[32]{0:T(128)S(1)} %add_rsqrt_fusion.4, f32[8192]{0:T(1024)S(1)} %bitcast.79, bf16[32,8192]{1,0:T(8,128)(2,1)S(1)} %collective-permute-done.1, bf16[128,8192]{1,0:T(8,128)(2,1)} %all-gather.3.cloned.1.call-done, ...), kind=kOutput, calls=%fused_computation.11 | convolution fusion | flops 539246592 | bytes 19432960 | tf_op jit(solution)/shard_map/dot_general | solution.py:31
  102.4 4.1 collective-permute-start.2
  106.6 9.0 %collective-permute-done.2 = bf16[32,8192]{1,0:T(8,128)(2,1)S(1)} collective-permute-done((bf16[32,8192]{1,0:T(8,128)(2,1)}, bf16[32,8192]{1,0:T(8,128)(2,1)S(1)}, u32[]{:S(2)}, u32[]{:S(2)}) %collective-permute-start.2) | collective-permute-done | bytes 524320 | tf_op jit(solution)/shard_map/ppermute | solution.py:14
  115.6 1.3 fusion.62
  116.9 9.1 %fusion.3 = bf16[32,8192]{1,0:T(8,128)(2,1)S(1)} fusion(bf16[1,512,8192]{2,1,0:T(8,128)(2,1)} %param.10, bf16[1,8192,512]{2,1,0:T(8,128)(2,1)} %param.9, f32[32]{0:T(128)S(1)} %add_rsqrt_fusion.3, f32[8192]{0:T(1024)S(1)} %bitcast.80, bf16[32,8192]{1,0:T(8,128)(2,1)S(1)} %collective-permute-done.2, bf16[128,8192]{1,0:T(8,128)(2,1)} %all-gather.3.cloned.1.call-done, ...), kind=kOutput, calls=%fused_computation.12 | convolution fusion | flops 539246592 | bytes 19432960 | tf_op jit(solution)/shard_map/dot_general | solution.py:31
  126.0 4.2 collective-permute-start.3
  130.2 7.6 %collective-permute-done.3 = bf16[32,8192]{1,0:T(8,128)(2,1)S(1)} collective-permute-done((bf16[32,8192]{1,0:T(8,128)(2,1)S(1)}, bf16[32,8192]{1,0:T(8,128)(2,1)S(1)}, u32[]{:S(2)}, u32[]{:S(2)}) %collective-permute-start.3) | collective-permute-done | bytes 524320 | tf_op jit(solution)/shard_map/ppermute | solution.py:14
  137.8 1.5 fusion.65
  139.3 9.3 %fusion.4 = bf16[32,8192]{1,0:T(8,128)(2,1)S(1)} fusion(bf16[1,512,8192]{2,1,0:T(8,128)(2,1)} %param.10, bf16[1,8192,512]{2,1,0:T(8,128)(2,1)} %param.9, f32[32]{0:T(128)S(1)} %add_rsqrt_fusion.2, f32[8192]{0:T(1024)S(1)} %bitcast.81, bf16[32,8192]{1,0:T(8,128)(2,1)} %copy-done.2, bf16[128,8192]{1,0:T(8,128)(2,1)} %all-gather.3.cloned.1.call-done, pred[]{:T(512)S(6)} %eq.5), kind=kOutput, calls=%fused_computation.13 | convolution fusion | flops 539246592 | bytes 19432576 | tf_op jit(solution)/shard_map/dot_general | solution.py:31
  148.6 4.3 collective-permute-start.4
  152.9 6.8 %collective-permute-done.4 = bf16[32,8192]{1,0:T(8,128)(2,1)S(1)} collective-permute-done((bf16[32,8192]{1,0:T(8,128)(2,1)S(1)}, bf16[32,8192]{1,0:T(8,128)(2,1)S(1)}, u32[]{:S(2)}, u32[]{:S(2)}) %collective-permute-start.4) | collective-permute-done | bytes 524320 | tf_op jit(solution)/shard_map/ppermute | solution.py:14
  159.7 0.8 copy-done.3
  160.5 1.3 fusion.68
  161.9 10.1 %fusion.5 = bf16[32,8192]{1,0:T(8,128)(2,1)} fusion(bf16[1,512,8192]{2,1,0:T(8,128)(2,1)} %param.10, bf16[1,8192,512]{2,1,0:T(8,128)(2,1)} %param.9, f32[32]{0:T(128)S(1)} %add_rsqrt_fusion.1, f32[8192]{0:T(1024)S(1)} %bitcast.82, bf16[32,8192]{1,0:T(8,128)(2,1)} %copy-done.3, bf16[128,8192]{1,0:T(8,128)(2,1)} %all-gather.3.cloned.1.call-done, pred[]{:T(512)S(6)} %eq.5), kind=kOutput, calls=%fused_computation.14 | convolution fusion | flops 539246592 | bytes 19432576 | tf_op jit(solution)/shard_map/dot_general | solution.py:31
  171.9 5.0 collective-permute-start.5
  177.0 5.6 collective-permute-done.5
  182.6 1.3 fusion.71
  183.9 10.1 %fusion.6 = bf16[32,8192]{1,0:T(8,128)(2,1)} fusion(bf16[1,512,8192]{2,1,0:T(8,128)(2,1)} %param.10, bf16[1,8192,512]{2,1,0:T(8,128)(2,1)} %param.9, f32[32]{0:T(128)S(1)} %add_rsqrt_fusion, f32[8192]{0:T(1024)S(1)} %bitcast.83, bf16[32,8192]{1,0:T(8,128)(2,1)} %collective-permute-done.5, bf16[128,8192]{1,0:T(8,128)(2,1)} %all-gather.3.cloned.1.call-done, ...), kind=kOutput, calls=%fused_computation.15 | convolution fusion | flops 539246592 | bytes 19432576 | tf_op jit(solution)/shard_map/dot_general | solution.py:31
  194.0 2.9 maximum_select_fusion
  197.0 66.7 %all-reduce.3.cloned.1.call-done = bf16[128,8192]{1,0:T(8,128)(2,1)} async-done(((bf16[128,8192]{1,0:T(8,128)(2,1)}), bf16[128,8192]{1,0:T(8,128)(2,1)}) %all-reduce.3.cloned.1.call-update) | async-done | bytes 2097168 | tf_op jit(solution)/shard_map/psum | solution.py:19
  263.7 1.9 constant_dynamic-slice_fusion
  265.7 73.6 %all-gather.5.cloned.1.call-done = bf16[4096,2048]{1,0:T(8,128)(2,1)} async-done(((bf16[128,2048]{1,0:T(8,128)(2,1)}), bf16[4096,2048]{1,0:T(8,128)(2,1)}) %all-gather.5.cloned.1.call-update) | async-done | bytes 16777232 | tf_op jit(solution)/shard_map/all_gather | solution.py:62
  339.3 14.4 %fusion.136 = f32[4096,512]{1,0:T(8,128)} fusion(bf16[4096,2048]{1,0:T(8,128)(2,1)} %all-gather.5.cloned.1.call-done, bf16[2048,512]{1,0:T(8,128)(2,1)S(1)} %copy-done), kind=kOutput, calls=%fused_computation.123 | convolution fusion | flops 8589934592 | bytes 27262976 | tf_op jit(solution)/shard_map/dot_general | solution.py:72
  353.7 0.6 copy-done.5
  354.3 0.6 broadcast_in_dim.11
  354.9 5.4 all-to-all-start.1
  360.3 5.6 copy.17
  365.9 1.3 all-to-all-done.1
  367.2 6.1 %all-to-all-start = ((bf16[128,32,512]{2,0,1:T(8,128)(2,1)}), bf16[128,32,512]{2,0,1:T(8,128)(2,1)}, u32[]{:S(2)}, u32[]{:S(2)}) async-start(bf16[128,32,512]{2,0,1:T(8,128)(2,1)} %bitcast.75), calls=%async_computation | async-start | bytes 8388608 | tf_op jit(solution)/shard_map/all_to_all | solution.py:66
  373.4 25.6 %gather_fusion.1 = bf16[4096]{0:T(1024)(128)(2,1)S(1)} fusion(bf16[4096]{0:T(1024)(128)(2,1)S(1)} %bitcast.74, s32[4096]{0:T(1024)S(1)} %fusion.132), kind=kCustom, calls=%fused_computation.1 | custom fusion | bytes 32768 | tf_op jit(solution)/shard_map/gather | solution.py:74
  399.0 26.5 %all-to-all-done = bf16[128,32,512]{2,0,1:T(8,128)(2,1)} async-done(((bf16[128,32,512]{2,0,1:T(8,128)(2,1)}), bf16[128,32,512]{2,0,1:T(8,128)(2,1)}, u32[]{:S(2)}, u32[]{:S(2)}) %all-to-all-start) | async-done | bytes 4194336 | tf_op jit(solution)/shard_map/all_to_all | solution.py:66
  425.5 20.1 %gather_fusion = bf16[4096,512]{1,0:T(8,128)(2,1)} fusion(bf16[4096,512]{1,0:T(8,128)(2,1)} %bitcast.4, s32[4096]{0:T(1024)S(1)} %fusion.132), kind=kCustom, calls=%fused_computation | custom fusion | bytes 8404992 | tf_op jit(solution)/shard_map/gather | solution.py:74
  445.7 67.7 %all-reduce.5.cloned.1.call-done = f32[4096,512]{1,0:T(8,128)} async-done(((f32[4096,512]{1,0:T(8,128)}), f32[4096,512]{1,0:T(8,128)}) %all-reduce.5.cloned.1.call-update) | async-done | bytes 8388624 | tf_op jit(solution)/shard_map/psum | solution.py:73
  513.4 6.7 %multiply_reduce_fusion = f32[]{:T(128)} fusion(f32[4096,512]{1,0:T(8,128)} %all-reduce.5.cloned.1.call-done, bf16[4096,512]{1,0:T(8,128)(2,1)} %gather_fusion, f32[4096]{0:T(1024)S(1)} %convert_element_type.153), kind=kLoop, calls=%fused_computation.37 | loop fusion | flops 10485759 | bytes 12599300 | tf_op jit(solution)/shard_map/reduce_sum | solution.py:76
  520.1 63.3 %psum.23 = f32[]{:T(128)} all-reduce(f32[]{:T(128)} %multiply_reduce_fusion), channel_id=1, replica_groups=mesh['dp'=32,'pipe'=4] {'dp'}, use_global_device_ids=true, to_apply=%region_10.11 | all-reduce | flops 1 | bytes 8 | tf_op jit(solution)/shard_map/psum | solution.py:76
  584.1 20.1 %fusion.31 = bf16[2048,512]{1,0:T(8,128)(2,1)} fusion(bf16[4096,2048]{1,0:T(8,128)(2,1)} %all-gather.5.cloned.1.call-done, f32[4096,512]{1,0:T(8,128)} %all-reduce.5.cloned.1.call-done, bf16[4096,512]{1,0:T(8,128)(2,1)} %gather_fusion, f32[4096]{0:T(1024)S(1)} %convert_element_type.153), kind=kOutput, calls=%fused_computation.44 | convolution fusion | flops 8601468928 | bytes 31473664 | tf_op jit(solution)/shard_map/dot_general | solution.py:78
  (27 shorter events, 0.3 us)
Async XLA Ops:
  7.2 332.1 %copy-start = (bf16[2048,512]{1,0:T(8,128)(2,1)S(1)}, bf16[2048,512]{1,0:T(8,128)(2,1)}, u32[]{:S(2)}) copy-start(bf16[2048,512]{1,0:T(8,128)(2,1)} %param.12) | copy-start | bytes 6291460
  7.2 36.8 %all-gather.3.cloned.1.call-start = ((), (), s32[]{:S(2)}) async-start(), calls=%async_computation.2 | async-start | bytes 2621440 | tf_op jit(solution)/shard_map/all_gather | solution.py:41
  7.9 255.8 %all-reduce.3.cloned.1.call-start = ((), (), s32[]{:S(2)}) async-start(), calls=%async_computation.3 | async-start | bytes 4194304 | tf_op jit(solution)/shard_map/psum | solution.py:19
  54.4 12.7 %collective-permute-start = (bf16[32,8192]{1,0:T(8,128)(2,1)S(1)}, bf16[32,8192]{1,0:T(8,128)(2,1)S(1)}, u32[]{:S(2)}, u32[]{:S(2)}) collective-permute-start(bf16[32,8192]{1,0:T(8,128)(2,1)S(1)} %fusion), channel_id=1, source_target_pairs={{0,1},{1,2},{2,3},{4,5},{5,6},{6,7},{8,9},{9,10},{10,11},{12,13},{... | collective-permute-start | bytes 1572872 | tf_op jit(solution)/shard_map/ppermute | solution.py:14
  77.5 13.8 %collective-permute-start.1 = (bf16[32,8192]{1,0:T(8,128)(2,1)S(1)}, bf16[32,8192]{1,0:T(8,128)(2,1)S(1)}, u32[]{:S(2)}, u32[]{:S(2)}) collective-permute-start(bf16[32,8192]{1,0:T(8,128)(2,1)S(1)} %fusion.1), channel_id=1, source_target_pairs={{0,1},{1,2},{2,3},{4,5},{5,6},{6,7},{8,9},{9,10},{10,11},{12,13},{... | collective-permute-start | bytes 1572872 | tf_op jit(solution)/shard_map/ppermute | solution.py:14
  102.4 13.1 %collective-permute-start.2 = (bf16[32,8192]{1,0:T(8,128)(2,1)}, bf16[32,8192]{1,0:T(8,128)(2,1)S(1)}, u32[]{:S(2)}, u32[]{:S(2)}) collective-permute-start(bf16[32,8192]{1,0:T(8,128)(2,1)} %fusion.2), channel_id=1, source_target_pairs={{0,1},{1,2},{2,3},{4,5},{5,6},{6,7},{8,9},{9,10},{10,11},{12,13},{... | collective-permute-start | bytes 1572872 | tf_op jit(solution)/shard_map/ppermute | solution.py:14
  126.0 11.8 %collective-permute-start.3 = (bf16[32,8192]{1,0:T(8,128)(2,1)S(1)}, bf16[32,8192]{1,0:T(8,128)(2,1)S(1)}, u32[]{:S(2)}, u32[]{:S(2)}) collective-permute-start(bf16[32,8192]{1,0:T(8,128)(2,1)S(1)} %fusion.3), channel_id=1, source_target_pairs={{0,1},{1,2},{2,3},{4,5},{5,6},{6,7},{8,9},{9,10},{10,11},{12,13},{... | collective-permute-start | bytes 1572872 | tf_op jit(solution)/shard_map/ppermute | solution.py:14
  137.8 1.5 copy-start.2
  148.6 11.1 %collective-permute-start.4 = (bf16[32,8192]{1,0:T(8,128)(2,1)S(1)}, bf16[32,8192]{1,0:T(8,128)(2,1)S(1)}, u32[]{:S(2)}, u32[]{:S(2)}) collective-permute-start(bf16[32,8192]{1,0:T(8,128)(2,1)S(1)} %fusion.4), channel_id=1, source_target_pairs={{0,1},{1,2},{2,3},{4,5},{5,6},{6,7},{8,9},{9,10},{10,11},{12,13},{... | collective-permute-start | bytes 1572872 | tf_op jit(solution)/shard_map/ppermute | solution.py:14
  159.7 0.8 copy-start.3
  171.9 10.7 %collective-permute-start.5 = (bf16[32,8192]{1,0:T(8,128)(2,1)}, bf16[32,8192]{1,0:T(8,128)(2,1)}, u32[]{:S(2)}, u32[]{:S(2)}) collective-permute-start(bf16[32,8192]{1,0:T(8,128)(2,1)} %fusion.5), channel_id=1, source_target_pairs={{0,1},{1,2},{2,3},{4,5},{5,6},{6,7},{8,9},{9,10},{10,11},{12,13},{... | collective-permute-start | bytes 1572872 | tf_op jit(solution)/shard_map/ppermute | solution.py:14
  196.9 142.3 %all-gather.5.cloned.1.call-start = ((), (), s32[]{:S(2)}) async-start(), calls=%async_computation.4 | async-start | bytes 17301504 | tf_op jit(solution)/shard_map/all_gather | solution.py:62
  265.6 247.8 %all-reduce.5.cloned.1.call-start = ((), (), s32[]{:S(2)}) async-start(), calls=%async_computation.5 | async-start | bytes 16777216 | tf_op jit(solution)/shard_map/psum | solution.py:73
  353.6 0.7 copy-start.5
  354.9 12.3 %all-to-all-start.1 = ((bf16[128,32,1]{0,2,1:T(2,128)(2,1)}), bf16[128,32,1]{0,2,1:T(2,128)(2,1)S(1)}, u32[]{:S(2)}, u32[]{:S(2)}) async-start(bf16[128,32,1]{0,2,1:T(2,128)(2,1)} %broadcast_in_dim.11), calls=%async_computation.1 | async-start | bytes 32768 | tf_op jit(solution)/shard_map/all_to_all | solution.py:67
  360.3 13.0 %copy-start.4 = (s32[4096]{0:T(1024)S(1)}, s32[4096]{0:T(1024)}, u32[]{:S(2)}) copy-start(s32[4096]{0:T(1024)} %param.15) | copy-start | bytes 49156
  367.2 58.4 %all-to-all-start = ((bf16[128,32,512]{2,0,1:T(8,128)(2,1)}), bf16[128,32,512]{2,0,1:T(8,128)(2,1)}, u32[]{:S(2)}, u32[]{:S(2)}) async-start(bf16[128,32,512]{2,0,1:T(8,128)(2,1)} %bitcast.75), calls=%async_computation | async-start | bytes 8388608 | tf_op jit(solution)/shard_map/all_to_all | solution.py:66
  584.1 20.1 %copy-start.1 = (bf16[2048,512]{1,0:T(8,128)(2,1)S(1)}, bf16[2048,512]{1,0:T(8,128)(2,1)}, u32[]{:S(2)}) copy-start(bf16[2048,512]{1,0:T(8,128)(2,1)} %param.12) | copy-start | bytes 6291460
Sparse Core Ops, SparseCore 0:
  9.7 34.2 all-gather.2
  197.1 66.6 all-reduce.2
  266.8 72.3 all-gather.4
  353.8 159.5 all-reduce.4
where the time goes:
time: 616 us; the launch traced here: 612 us
  waiting for transfers between devices  321 us (52%)
  matrix products  101 us (16%)
  blocking collectives  63.3 us (10%)
  local copies, waits for them, and re-layouts  55.3 us (9%)
  starting transfers between devices  35.6 us (6%)
  other arithmetic  19.9 us (3%)
  between operations  15.7 us (3%)
    all_gather x1, waiting for transfers between devices, shards(): gathered = lax.all_gather(my_features, 'dp', axis=0, tiled=True)  73.6 us
    psum x1, waiting for transfers between devices, shards(): output = lax.psum(partial_out, 'pipe')  67.7 us
    psum x1, waiting for transfers between devices, from_root(): return lax.psum(block, axis)  66.7 us
    dot_general x7, matrix products, apply_layer(): branch = jnp.dot(values, w_out, preferred_element_type=jnp.float32)  66.5 us
    psum x1, blocking collectives, shards(): total = lax.psum(jnp.sum(diff * diff), 'dp')  63.3 us
    ppermute x6, waiting for transfers between devices, from_behind(): return lax.ppermute(block, axis, route)  49.2 us
    all_gather x1, waiting for transfers between devices, shards(): full_in = lax.all_gather(student_in, 'pipe', axis=1, tiled=True)  35.2 us
    all_to_all x1, waiting for transfers between devices, shards(): lax.all_to_all(teacher_codes, 'dp', split_axis=1, concat_axis=0, tiled=True)  26.5 us
  transfers between devices with their start and end apart: 12, of which 12 were waited for; matrix products, arithmetic and copies ran while one was open for 9% of the time, Pallas kernels for 0%

commit v1 on v0

v1 whole, which is shorter than its diff:
```python
import functools
import math

import jax
import jax.numpy as jnp
from jax import lax
from jax.experimental import pallas as pl
from jax.experimental.pallas import tpu as pltpu
from jax.sharding import PartitionSpec as P

MESH = pl.DeviceIdType.MESH
SIDE = 4
CHIPS = SIDE * SIDE


def place(dp):
    core = lax.rem(dp, 2)
    chip = dp // 2
    return chip // SIDE, lax.rem(chip, SIDE), core


def cycle_position(x, y, core):
    return SIDE * (y + core * (x - y)) + lax.rem(x + y, SIDE)


def cycle_device(position, core):
    major = position // SIDE
    minor = lax.rem(lax.rem(position, SIDE) - major + SIDE, SIDE)
    x = minor + core * (major - minor)
    y = major + core * (minor - major)
    return (x * SIDE + y) * 2 + core


def wide_kernel(
    inv_root,
    h_ref,
    proj_ref,
    target_ref,
    grad_ref,
    loss_ref,
    held,
    total,
    y_own,
    y_keep,
    out1,
    in1,
    out2,
    in2,
    rows_g,
    own_sem,
    ring_send,
    ring_recv,
    side_send,
    side_recv,
    sum1_send,
    sum1_recv,
    sum2_send,
    sum2_recv,
    rows1_send,
    rows1_recv,
    rows2_send,
    rows2_recv,
):
    dp = lax.axis_index("dp")
    z = lax.axis_index("pipe")
    x, y, core = place(dp)
    here = cycle_position(x, y, core)
    after = cycle_device(lax.rem(here + 1, CHIPS), core)
    before = cycle_device(lax.rem(here + CHIPS - 1, CHIPS), core)
    sibling = dp + 1 - 2 * core
    za = z + 1 - 2 * lax.rem(z, 2)
    zb = 3 - z
    steps = CHIPS
    part = h_ref.shape[0] // 2
    block = 4 * part
    half = block // 2
    zpair = (za, zb)
    ring = (after, before)

    barrier = pltpu.get_barrier_semaphore()
    for device in ((after, z), (before, z), (sibling, z), (dp, za), (dp, zb)):
        pl.semaphore_signal(barrier, inc=1, device_id=device, device_id_type=MESH)
    pl.semaphore_wait(barrier, 5)

    mine = pl.multiple_of(core * 2 * part, 2 * part)
    theirs = pl.multiple_of((1 - core) * 2 * part, 2 * part)

    def own_copy():
        return pltpu.make_async_copy(h_ref, held.at[0, pl.ds(mine, 2 * part)], own_sem)

    def ring_copy(s, way):
        rows = pl.ds(pl.multiple_of(mine + way * part, part), part)
        return pltpu.make_async_remote_copy(
            src_ref=held.at[s, rows],
            dst_ref=held.at[s + 1, rows],
            send_sem=ring_send.at[s, way],
            recv_sem=ring_recv.at[s + 1, way],
            device_id=(ring[way], z),
            device_id_type=MESH,
        )

    def ring_arrival(s, way):
        rows = pl.ds(pl.multiple_of(mine + way * part, part), part)
        return pltpu.make_async_remote_copy(
            src_ref=held.at[s, rows],
            dst_ref=held.at[s, rows],
            send_sem=ring_send.at[s, way],
            recv_sem=ring_recv.at[s, way],
            device_id=(ring[way], z),
            device_id_type=MESH,
        )

    def side_copy(s, way, start):
        rows = pl.ds(pl.multiple_of(start + way * part, part), part)
        return pltpu.make_async_remote_copy(
            src_ref=held.at[s, rows],
            dst_ref=held.at[s, rows],
            send_sem=side_send.at[s, way],
            recv_sem=side_recv.at[s, way],
            device_id=(sibling, z),
            device_id_type=MESH,
        )

    def sum1_copy(s, k):
        return pltpu.make_async_remote_copy(
            src_ref=out1.at[s, k],
            dst_ref=in1.at[s, k],
            send_sem=sum1_send.at[s, k],
            recv_sem=sum1_recv.at[s, k],
            device_id=(dp, zpair[k]),
            device_id_type=MESH,
        )

    def sum2_copy(s, k):
        return pltpu.make_async_remote_copy(
            src_ref=out2.at[s, k],
            dst_ref=in2.at[s, k],
            send_sem=sum2_send.at[s, k],
            recv_sem=sum2_recv.at[s, k],
            device_id=(dp, zpair[1 - k]),
            device_id_type=MESH,
        )

    def rows1_copy(s, k, quarter):
        return pltpu.make_async_remote_copy(
            src_ref=rows_g.at[s, quarter],
            dst_ref=rows_g.at[s, quarter],
            send_sem=rows1_send.at[s, k],
            recv_sem=rows1_recv.at[s, k],
            device_id=(dp, zpair[k]),
            device_id_type=MESH,
        )

    def rows2_copy(s, k, quarter):
        rows = pl.ds(k * half, half)
        return pltpu.make_async_remote_copy(
            src_ref=rows_g.at[s, quarter, rows],
            dst_ref=rows_g.at[s, quarter, rows],
            send_sem=rows2_send.at[s, k],
            recv_sem=rows2_recv.at[s, k],
            device_id=(dp, zpair[k]),
            device_id_type=MESH,
        )

    loss_ref[...] = jnp.zeros_like(loss_ref)
    total[...] = jnp.zeros_like(total)
    own_copy().start()
    own_copy().wait()

    def body(i, carry):
        @pl.when(i < steps)
        def _():
            @pl.when(i > 0)
            def _():
                for way in range(2):
                    ring_arrival(i, way).wait_recv()

            @pl.when(i < steps - 1)
            def _():
                for way in range(2):
                    ring_copy(i, way).start()

            for way in range(2):
                side_copy(i, way, mine).start()

        @pl.when(jnp.logical_and(i >= 1, i < steps + 1))
        def _():
            s = i - 1
            slot = lax.rem(s, 2)
            for k in range(2):
                rows = pl.ds(k * half, half)
                sum1_copy(s, k).wait_recv()
                passed = y_own[slot, zpair[1 - k], rows, :] + in1[s, k, 1].astype(jnp.float32)
                out2[s, k] = passed.astype(jnp.bfloat16)
                sum2_copy(s, k).start()
                y_keep[slot, rows, :] = y_own[slot, z, rows, :] + in1[s, k, 0].astype(jnp.float32)

        @pl.when(jnp.logical_and(i >= 2, i < steps + 2))
        def _():
            s = i - 2
            slot = lax.rem(s, 2)
            for k in range(2):
                sum2_copy(s, k).wait_recv()
            for chunk in range(4):
                ring_core, way = chunk // 2, chunk % 2
                at = cycle_position(x, y, ring_core)
                origin = cycle_device(lax.rem(at + (CHIPS - s if way == 0 else s), CHIPS), ring_core)
                token = pl.multiple_of((origin * 2 + way) * part, part)
                rows = pl.ds(chunk * part, part)
                inside = pl.ds((chunk % 2) * part, part)
                diff = (
                    y_keep[slot, rows, :]
                    + in2[s, chunk // 2, inside, :].astype(jnp.float32)
                    - target_ref[pl.ds(token, part), :]
                )
                rows_g[s, z, rows, :] = (diff * inv_root).astype(jnp.bfloat16)
                loss_ref[...] += jnp.sum((diff * diff).reshape(part // 8, 8, diff.shape[1]), axis=0)
            for k in range(2):
                rows1_copy(s, k, z).start()

        @pl.when(jnp.logical_and(i >= 3, i < steps + 3))
        def _():
            s = i - 3
            for k in range(2):
                rows1_copy(s, k, zpair[k]).wait_recv()
            for k in range(2):
                rows2_copy(s, k, zpair[1 - k]).start()

        @pl.when(i < steps)
        def _():
            slot = lax.rem(i, 2)
            for way in range(2):
                side_copy(i, way, theirs).wait_recv()
            for n in range(2):
                part_y = jnp.dot(
                    held[i], proj_ref[:, n * 256 : (n + 1) * 256], preferred_element_type=jnp.float32
                )
                y_own[slot, 2 * n] = part_y[:, :128]
                y_own[slot, 2 * n + 1] = part_y[:, 128:]
            for k in range(2):
                rows = pl.ds(k * half, half)
                other = 3 - zpair[k] if k == 0 else zpair[k] + 1 - 2 * lax.rem(zpair[k], 2)
                out1[i, k, 0] = y_own[slot, zpair[k], rows, :].astype(jnp.bfloat16)
                out1[i, k, 1] = y_own[slot, other, rows, :].astype(jnp.bfloat16)
                sum1_copy(i, k).start()

        @pl.when(i >= 4)
        def _():
            s = i - 4
            for k in range(2):
                rows2_copy(s, k, 3 - zpair[k] if k == 0 else zpair[k] + 1 - 2 * lax.rem(zpair[k], 2)).wait_recv()
            rows = jnp.concatenate([rows_g[s, q] for q in range(4)], axis=1)
            for f in range(8):
                features = slice(f * 256, (f + 1) * 256)
                total[features, :] += lax.dot_general(
                    held[s, :, features], rows, (((0,), (0,)), ((), ())), preferred_element_type=jnp.float32
                )

        return carry

    lax.fori_loop(0, steps + 4, body, 0)

    def finish(s, carry):
        @pl.when(s < steps - 1)
        def _():
            for way in range(2):
                ring_copy(s, way).wait_send()

        for k in range(2):
            side_copy(s, k, mine).wait_send()
            sum1_copy(s, k).wait_send()
            sum2_copy(s, k).wait_send()
            rows1_copy(s, k, z).wait_send()
            rows2_copy(s, k, zpair[1 - k]).wait_send()
        return carry

    lax.fori_loop(0, steps, finish, 0)
    grad_ref[...] = total[...].astype(jnp.bfloat16)


def wide(hidden, proj, target, inv_root):
    rows, features = hidden.shape
    columns = proj.shape[1]
    quarter = columns // 4
    block = 2 * rows
    half = block // 2
    pairs = pltpu.SemaphoreType.DMA((CHIPS, 2))
    vmem = pl.BlockSpec(memory_space=pltpu.VMEM)
    return pl.pallas_call(
        functools.partial(wide_kernel, inv_root),
        out_shape=(
            jax.ShapeDtypeStruct((features, columns), jnp.bfloat16),
            jax.ShapeDtypeStruct((8, quarter), jnp.float32),
        ),
        in_specs=[vmem] * 3,
        out_specs=(vmem, vmem),
        scratch_shapes=[
            pltpu.VMEM((CHIPS, block, features), jnp.bfloat16),
            pltpu.VMEM((features, columns), jnp.float32),
            pltpu.VMEM((2, 4, block, quarter), jnp.float32),
            pltpu.VMEM((2, block, quarter), jnp.float32),
            pltpu.VMEM((CHIPS, 2, 2, half, quarter), jnp.bfloat16),
            pltpu.VMEM((CHIPS, 2, 2, half, quarter), jnp.bfloat16),
            pltpu.VMEM((CHIPS, 2, half, quarter), jnp.bfloat16),
            pltpu.VMEM((CHIPS, 2, half, quarter), jnp.bfloat16),
            pltpu.VMEM((CHIPS, 4, block, quarter), jnp.bfloat16),
            pltpu.SemaphoreType.DMA,
        ]
        + [pairs] * 12,
        compiler_params=pltpu.CompilerParams(
            collective_id=0, has_side_effects=True, vmem_limit_bytes=56 * 1024 * 1024
        ),
    )(hidden, proj, target)


def shards(
    student_in, value_weight, folded_out, norm_gain, proj, teacher_codes, teacher_scales, perm
):
    sections = lax.axis_size("pipe")
    section = lax.axis_index("pipe")
    n_ranks = lax.axis_size("dp")
    rank = lax.axis_index("dp")
    rows, features = student_in.shape
    width = features * sections
    head = value_weight.shape[2]
    tokens = rows * n_ranks
    columns = proj.shape[1]
    total_cols = columns * n_ranks

    scaled = value_weight[0].astype(jnp.float32) * norm_gain[0].astype(jnp.float32)[:, None]
    w_value = scaled.astype(jnp.bfloat16).reshape(sections, n_ranks, features // n_ranks, head)
    w_value = lax.dynamic_index_in_dim(w_value, rank, 1, keepdims=False)
    w_value = lax.all_to_all(w_value, "pipe", split_axis=0, concat_axis=0, tiled=True)
    w_value = lax.all_gather(w_value, "dp", axis=1, tiled=True)
    w_out = lax.dynamic_slice_in_dim(folded_out[0], rank * (head // n_ranks), head // n_ranks, 0)
    w_out = w_out.reshape(head // n_ranks, sections, features).transpose(1, 0, 2)
    w_out = lax.all_to_all(w_out, "pipe", split_axis=0, concat_axis=0, tiled=True)
    w_out = lax.all_gather(w_out, "dp", axis=1, tiled=True)

    codes = teacher_codes.reshape(rows, n_ranks, sections, columns // sections)
    codes = lax.dynamic_index_in_dim(codes, section, 2, keepdims=False)
    codes = lax.all_to_all(codes, "dp", split_axis=1, concat_axis=0, tiled=True).reshape(tokens, -1)
    scales = lax.all_gather(teacher_scales, "dp", axis=0, tiled=True)
    target = codes[perm].astype(jnp.float32) * scales[perm].astype(jnp.float32)[:, None]

    hidden = student_in
    for layer in range(sections):
        wide_rows = hidden.astype(jnp.float32)
        squares = jnp.sum(wide_rows * wide_rows, axis=1, keepdims=True)
        products = jnp.dot(hidden, w_value[layer], preferred_element_type=jnp.float32)
        both = lax.psum(jnp.concatenate([products, jnp.broadcast_to(squares, (rows, 128))], axis=1), "pipe")
        scale = lax.rsqrt(both[:, head : head + 1] / width + 1e-05)
        values = (both[:, :head] * scale).astype(jnp.bfloat16)
        branch = jnp.dot(values, w_out[layer], preferred_element_type=jnp.float32)
        hidden = (wide_rows + branch).astype(jnp.bfloat16)

    grad_proj, squared = wide(hidden, proj, target, 1.0 / math.sqrt(tokens))
    loss = 0.5 * lax.psum(jnp.sum(squared), ("dp", "pipe")) / (tokens * total_cols)
    return (grad_proj, loss)


def solution(mesh):
    return jax.shard_map(
        shards,
        mesh=mesh,
        in_specs=(
            P("dp", "pipe"),
            P("pipe", None, None),
            P("pipe", None, None),
            P("pipe", None),
            P("pipe", "dp"),
            P("dp", None),
            P("dp"),
            P(),
        ),
        out_specs=(P("pipe", "dp"), P()),
        check_vma=False,
    )
```

time: 616 us -> 541 us (0.88)
  waiting for transfers between devices: 321 us -> 165 us
  Pallas kernels: 0 us -> 119 us
  matrix products: 101 us -> 25.6 us
  blocking collectives: 63.3 us -> 107 us
  local copies, waits for them, and re-layouts: 55.3 us -> 85.7 us
  starting transfers between devices: 35.6 us -> 10.2 us
  other arithmetic: 19.9 us -> 11.2 us
    pallas_call x0 -> x1, Pallas kernels: none -> 119 us  [wide(): pl.pallas_call(functools.partial(wide_kernel, inv_root), out_shape=(jax.S...]
    dot_general x9 -> x8, matrix products: 101 us -> 25.6 us  [the longest x4 15.7 us: shards(): branch = jnp.dot(values, w_out[layer], preferred_element_type=jnp.float32)]
    psum x2 -> x4, waiting for transfers between devices: 134 us -> 69.7 us  [shards(): lax.psum(jnp.concatenate([products, jnp.broadcast_to(squares, (rows, 128)...]
    ppermute x6 -> x0, waiting for transfers between devices: 49.2 us -> none  [from_behind(): return lax.ppermute(block, axis, route)]
    slice x0 -> x1, local copies, waits for them, and re-layouts: none -> 27.9 us  [shards(): branch = jnp.dot(values, w_out[layer], preferred_element_type=jnp.float32)]
    all_to_all x2 -> x1, waiting for transfers between devices: 27.8 us -> 0.01 us  [shards(): lax.all_to_all(codes, 'dp', split_axis=1, concat_axis=0, tiled=True)]
    ppermute x6 -> x0, starting transfers between devices: 23.9 us -> none  [from_behind(): return lax.ppermute(block, axis, route)]
    all_gather x0 -> x1, blocking collectives: none -> 23.3 us  [shards(): scales = lax.all_gather(teacher_scales, 'dp', axis=0, tiled=True)]
  transfers between devices with their start and end apart: 12 -> 7, of which waited for: 12 -> 5; matrix products, arithmetic and copies ran while one was open for 9% -> 18% of each run, Pallas kernels for 0% -> 0%
where the time goes in v1:
time: 541 us; the launch traced here: 540 us
  waiting for transfers between devices  165 us (30%)
  Pallas kernels  119 us (22%)
  blocking collectives  107 us (20%)
  local copies, waits for them, and re-layouts  85.7 us (16%)
  matrix products  25.6 us (5%)
  between operations  16.1 us (3%)
  other arithmetic  11.2 us (2%)
  starting transfers between devices  10.2 us (2%)
    pallas_call x1, Pallas kernels, wide(): pl.pallas_call(functools.partial(wide_kernel, inv_root), out_shape=(jax.S...  119 us
    psum x4, waiting for transfers between devices, shards(): lax.psum(jnp.concatenate([products, jnp.broadcast_to(squares, (rows, 128)...  69.7 us
    psum x1, blocking collectives, shards(): lax.psum(jnp.sum(squared), ('dp', 'pipe'))  64.3 us
    all_gather x1, waiting for transfers between devices, shards(): w_out = lax.all_gather(w_out, 'dp', axis=1, tiled=True)  51.5 us
    all_gather x1, waiting for transfers between devices, shards(): w_value = lax.all_gather(w_value, 'dp', axis=1, tiled=True)  43.9 us
    slice x1, local copies, waits for them, and re-layouts, shards(): branch = jnp.dot(values, w_out[layer], preferred_element_type=jnp.float32)  27.9 us
    gather x1, local copies, waits for them, and re-layouts, shards(): scales[perm].astype(jnp.float32)[:, None]  25.6 us
    all_gather x1, blocking collectives, shards(): scales = lax.all_gather(teacher_scales, 'dp', axis=0, tiled=True)  23.3 us
  transfers between devices with their start and end apart: 7, of which 5 were waited for; matrix products, arithmetic and copies ran while one was open for 18% of the time, Pallas kernels for 0%

profile of v1, /device:TPU:1, one launch (start us, length us, event | category | flops | bytes accessed | tf_op | source)
XLA Modules:
  0.0 540.2 jit_solution(16550222771489325822)
XLA Ops:
  7.2 0.9 convert_reduce_fusion
  8.1 0.1 reshape.43
  8.2 1.1 fusion.14
  9.3 11.3 %all_to_all.25 = bf16[4,64,512]{2,1,0:T(8,128)(2,1)} all-to-all(bf16[4,64,512]{2,1,0:T(8,128)(2,1)S(1)} %fusion.14), channel_id=1, replica_groups=mesh['dp'=32,'pipe'=4] {'pipe'}, dimensions={0} | all-to-all | bytes 524288 | tf_op jit(solution)/shard_map/all_to_all | solution.py:333
  20.6 0.0 all-gather.6.cloned.1.call-start
  20.7 1.0 constant_dynamic-slice_fusion.1
  21.7 0.2 reshape.39
  21.8 0.2 copy.22
  22.0 7.9 %all_to_all.26 = bf16[4,16,2048]{2,1,0:T(8,128)(2,1)S(1)} all-to-all(bf16[4,16,2048]{2,1,0:T(8,128)(2,1)S(1)} %copy.22), channel_id=1, replica_groups=mesh['dp'=32,'pipe'=4] {'pipe'}, dimensions={0} | all-to-all | bytes 524288 | tf_op jit(solution)/shard_map/all_to_all | solution.py:337
  29.9 0.9 copy.23
  30.8 0.0 all-reduce.5.cloned.1.call-start
  30.9 0.2 fusion.9
  31.1 43.9 %all-gather.4.cloned.1.call-done = bf16[4,2048,512]{2,1,0:T(8,128)(2,1)} async-done(((bf16[4,64,512]{2,1,0:T(8,128)(2,1)}), bf16[4,2048,512]{2,1,0:T(8,128)(2,1)}) %all-gather.4.cloned.1.call-update) | async-done | bytes 8388624 | tf_op jit(solution)/shard_map/all_gather | solution.py:334
  75.0 2.3 fusion.8
  77.3 0.7 pad_maximum_fusion
  78.1 51.5 %all-gather.6.cloned.1.call-done = bf16[4,512,2048]{2,0,1:T(4,128)(2,1)} async-done(((bf16[4,16,2048]{2,0,1:T(4,128)(2,1)}), bf16[4,512,2048]{2,0,1:T(4,128)(2,1)}) %all-gather.6.cloned.1.call-update) | async-done | bytes 8388624 | tf_op jit(solution)/shard_map/all_gather | solution.py:338
  129.6 27.9 %fusion.40 = (bf16[1,512,2048]{2,0,1:T(2,128)(2,1)}, bf16[1,512,2048]{2,0,1:T(2,128)(2,1)}, bf16[1,512,2048]{2,0,1:T(2,128)(2,1)}, bf16[1,512,2048]{2,0,1:T(2,128)(2,1)}) fusion(bf16[4,512,2048]{2,0,1:T(4,128)(2,1)} %all-gather.6.cloned.1.call-done), kind=kLoop, calls=%fused_computation.74 | loop fusion | bytes 16777216 | tf_op jit(solution)/shard_map/slice | solution.py:354
  157.6 14.3 %all-reduce.5.cloned.1.call-done = f32[128,640]{0,1:T(8,128)} async-done(((f32[128,640]{0,1:T(8,128)}), f32[128,640]{0,1:T(8,128)}) %all-reduce.5.cloned.1.call-update) | async-done | bytes 327696 | tf_op jit(solution)/shard_map/psum | solution.py:351
  171.9 0.7 fusion.39
  172.6 3.7 fusion.10
  176.3 2.5 fusion.6
  178.9 0.8 pad_maximum_fusion.1
  179.7 7.8 %reshape.40 = bf16[128,32,4,128]{3,2,1,0:T(4,128)(2,1)} reshape(bf16[128,16384]{1,0:T(8,128)(2,1)} %param.13) | data formatting | bytes 8388608 | tf_op jit(solution)/shard_map/reshape | solution.py:340
  187.5 4.7 constant_dynamic-slice_fusion
  192.1 2.2 copy.54
  194.3 9.7 %all-to-all-start.2 = ((bf16[128,32,128]{2,0,1:T(8,128)(2,1)}), bf16[128,32,128]{2,0,1:T(8,128)(2,1)S(1)}, u32[]{:S(2)}, u32[]{:S(2)}) async-start(bf16[128,32,128]{2,0,1:T(8,128)(2,1)} %bitcast.60), calls=%async_computation.2 | async-start | bytes 2097152 | tf_op jit(solution)/shard_map/all_to_all | solution.py:342
  204.1 0.2 all-reduce.9.cloned.1.call-start
  204.3 18.8 %all-reduce.7.cloned.1.call-done = f32[128,640]{0,1:T(8,128)} async-done(((f32[128,640]{0,1:T(8,128)}), f32[128,640]{0,1:T(8,128)}) %all-reduce.7.cloned.1.call-update) | async-done | bytes 327696 | tf_op jit(solution)/shard_map/psum | solution.py:351
  223.1 0.7 fusion.36
  223.8 3.8 fusion.11
  227.6 2.5 fusion.5
  230.1 0.8 pad_maximum_fusion.2
  231.0 23.3 %all-gather = bf16[32,1,128]{2,1,0:T(2,128)(2,1)S(1)} all-gather(bf16[1,1,128]{2,1,0:T(2,128)(2,1)S(1)} %bitcast.65), channel_id=1, replica_groups=mesh['dp'=32,'pipe'=4] {'dp'}, dimensions={0}, use_global_device_ids=true | all-gather | bytes 8448 | tf_op jit(solution)/shard_map/all_gather | solution.py:343
  254.3 0.1 reduce.1
  254.4 25.6 %gather_fusion.1 = bf16[4096]{0:T(1024)(128)(2,1)S(1)} fusion(bf16[4096]{0:T(1024)(128)(2,1)S(1)} %bitcast.61, s32[4096]{0:T(1024)S(1)} %fusion.27), kind=kCustom, calls=%fused_computation.1 | custom fusion | bytes 32768 | tf_op jit(solution)/shard_map/gather | solution.py:344
  280.0 12.1 %gather_fusion = bf16[4096,128]{1,0:T(8,128)(2,1)S(1)} fusion(bf16[4096,128]{1,0:T(8,128)(2,1)S(1)} %bitcast.62, s32[4096]{0:T(1024)S(1)} %fusion.27), kind=kCustom, calls=%fused_computation | custom fusion | bytes 2113536 | tf_op jit(solution)/shard_map/gather | solution.py:344
  292.2 0.7 fusion.33
  292.9 3.7 fusion.12
  296.6 2.5 fusion.4
  299.2 0.7 pad_maximum_fusion.3
  299.9 1.9 convert_multiply_fusion.target_ref
  301.9 36.6 %all-reduce.11.cloned.1.call-done = f32[128,640]{0,1:T(8,128)} async-done(((f32[128,640]{0,1:T(8,128)}), f32[128,640]{0,1:T(8,128)}) %all-reduce.11.cloned.1.call-update) | async-done | bytes 327696 | tf_op jit(solution)/shard_map/psum | solution.py:351
  338.4 0.7 fusion.30
  339.1 4.5 fusion.3.h_ref
  343.6 119.4 %shard_map.95 = (bf16[2048,512]{1,0:T(8,128)(2,1)}, f32[8,128]{1,0:T(8,128)}) custom-call(bf16[128,2048]{1,0:T(8,128)(2,1)} %fusion.3.h_ref, bf16[2048,512]{1,0:T(8,128)(2,1)} %proj_ref.1, f32[4096,128]{1,0:T(8,128)} %convert_multiply_fusion.target_ref), custom_call_target="tpu_custom_call" | custom-call | tf_op jit(solution)/shard_map/pallas_call | solution.py:289
  462.9 1.3 reduce_sum.49
  464.2 64.3 %psum.39 = f32[]{:T(128)} all-reduce(f32[]{:T(128)} %reduce_sum.49), channel_id=1, replica_groups=mesh['dp'=32,'pipe'=4] {'dp','pipe'}, use_global_device_ids=true, to_apply=%region_9.10 | all-reduce | flops 1 | bytes 8 | tf_op jit(solution)/shard_map/psum | solution.py:358
  529.1 3.0 copy.60
  (24 shorter events, 0.3 us)
Async XLA Ops:
  7.2 23.7 %copy-start = (bf16[128,2048]{1,0:T(8,128)(2,1)S(1)}, bf16[128,2048]{1,0:T(8,128)(2,1)}, u32[]{:S(2)}) copy-start(bf16[128,2048]{1,0:T(8,128)(2,1)} %param.8) | copy-start | bytes 1572868
  7.2 67.8 %all-gather.4.cloned.1.call-start = ((), (), s32[]{:S(2)}) async-start(), calls=%async_computation.3 | async-start | bytes 8650752 | tf_op jit(solution)/shard_map/all_gather | solution.py:334
  20.6 109.0 %all-gather.6.cloned.1.call-start = ((), (), s32[]{:S(2)}) async-start(), calls=%async_computation.5 | async-start | bytes 8650752 | tf_op jit(solution)/shard_map/all_gather | solution.py:338
  30.8 141.0 %all-reduce.5.cloned.1.call-start = ((), (), s32[]{:S(2)}) async-start(), calls=%async_computation.4 | async-start | bytes 655360 | tf_op jit(solution)/shard_map/psum | solution.py:351
  78.1 145.1 %all-reduce.7.cloned.1.call-start = ((), (), s32[]{:S(2)}) async-start(), calls=%async_computation.6 | async-start | bytes 655360 | tf_op jit(solution)/shard_map/psum | solution.py:351
  194.3 85.7 %all-to-all-start.2 = ((bf16[128,32,128]{2,0,1:T(8,128)(2,1)}), bf16[128,32,128]{2,0,1:T(8,128)(2,1)S(1)}, u32[]{:S(2)}, u32[]{:S(2)}) async-start(bf16[128,32,128]{2,0,1:T(8,128)(2,1)} %bitcast.60), calls=%async_computation.2 | async-start | bytes 2097152 | tf_op jit(solution)/shard_map/all_to_all | solution.py:342
  204.1 26.9 %copy-start.2 = (bf16[128]{0:T(256)(128)(2,1)S(1)}, bf16[128]{0:T(256)(128)(2,1)}, u32[]{:S(2)}) copy-start(bf16[128]{0:T(256)(128)(2,1)} %param.14) | copy-start | bytes 772
  204.1 50.3 %copy-start.1 = (s32[4096]{0:T(1024)S(1)}, s32[4096]{0:T(1024)}, u32[]{:S(2)}) copy-start(s32[4096]{0:T(1024)} %param.15) | copy-start | bytes 49156
  204.1 88.1 %all-reduce.9.cloned.1.call-start = ((), (), s32[]{:S(2)}) async-start(), calls=%async_computation.7 | async-start | bytes 655360 | tf_op jit(solution)/shard_map/psum | solution.py:351
  230.9 107.5 %all-reduce.11.cloned.1.call-start = ((), (), s32[]{:S(2)}) async-start(), calls=%async_computation.8 | async-start | bytes 655360 | tf_op jit(solution)/shard_map/psum | solution.py:351
Sparse Core Ops, SparseCore 0:
  20.7 54.1 all-gather.3
  77.2 52.3 all-gather.5
  132.6 39.2 all-reduce.4
  179.8 43.2 all-reduce.6
  231.0 41.7 all-reduce.8
  300.1 38.3 all-reduce.10

commit v2 on v1

--- a/solution.py
+++ b/solution.py
@@ -11,6 +11,8 @@
 MESH = pl.DeviceIdType.MESH
 SIDE = 4
 CHIPS = SIDE * SIDE
+RANKS = 2 * CHIPS
+LANES = 128
 
 
 def place(dp):
@@ -31,11 +33,374 @@
     return (x * SIDE + y) * 2 + core
 
 
+def layers_kernel(
+    eps,
+    h_ref,
+    value_ref,
+    out_ref,
+    gain_ref,
+    codes_ref,
+    scale_ref,
+    hidden_ref,
+    store_ref,
+    w_value,
+    w_out,
+    gains,
+    products,
+    normed,
+    values,
+    out1,
+    in1,
+    out2,
+    in2,
+    stage,
+    staged,
+    own_sem,
+    first_send,
+    ring_send,
+    ring_recv,
+    side_send,
+    side_recv,
+    gain_send,
+    gain_recv,
+    sum1_send,
+    sum1_recv,
+    sum2_send,
+    sum2_recv,
+    stage_sem,
+    code_send,
+    code_recv,
+):
+    dp = lax.axis_index("dp")
+    z = lax.axis_index("pipe")
+    x, y, core = place(dp)
+    here = cycle_position(x, y, core)
+    after = cycle_device(lax.rem(here + 1, CHIPS), core)
+    before = cycle_device(lax.rem(here + CHIPS - 1, CHIPS), core)
+    sibling = dp + 1 - 2 * core
+    zpair = (z + 1 - 2 * lax.rem(z, 2), 3 - z)
+    ring = (after, before)
+    rows, features = h_ref.shape
+    head = value_ref.shape[1]
+    half = rows // 2
+    weights = (w_value, w_out)
+    depth = (features // RANKS, head // RANKS)
+    width = 4 * features
+
+    barrier = pltpu.get_barrier_semaphore()
+
+    def greet(j, carry):
+        pl.semaphore_signal(
+            barrier, inc=1, device_id=(lax.rem(dp + j, RANKS), z), device_id_type=MESH
+        )
+        return carry
+
+    lax.fori_loop(1, RANKS, greet, 0)
+    for j in range(1, 4):
+        pl.semaphore_signal(
+            barrier, inc=1, device_id=(dp, lax.rem(z + j, 4)), device_id_type=MESH
+        )
+    pl.semaphore_wait(barrier, RANKS + 2)
+
+    def piece(kind, owner):
+        return pl.ds(pl.multiple_of(owner * depth[kind], depth[kind]), depth[kind])
+
+    def first_copy(kind, j):
+        to = lax.rem(z + j, 4)
+        if kind == 0:
+            start = pl.multiple_of(to * features + dp * depth[0], depth[0])
+            source = value_ref.at[pl.ds(start, depth[0])]
+        else:
+            source = out_ref.at[piece(1, dp), pl.ds(pl.multiple_of(to * features, features), features)]
+        return pltpu.make_async_remote_copy(
+            src_ref=source,
+            dst_ref=weights[kind].at[4 - j, piece(kind, dp)],
+            send_sem=first_send.at[kind, j - 1],
+            recv_sem=ring_recv.at[0, kind, 3 - j],
+            device_id=(dp, to),
+            device_id_type=MESH,
+        )
+
+    def gain_copy(j):
+        to = lax.rem(z + j, 4)
+        return pltpu.make_async_remote_copy(
+            src_ref=gain_ref.at[to],
+            dst_ref=gains.at[4 - j],
+            send_sem=gain_send.at[j - 1],
+            recv_sem=gain_recv.at[3 - j],
+            device_id=(dp, to),
+            device_id_type=MESH,
+        )
+
+    def origin(s, kind):
+        return cycle_device(lax.rem(here + (CHIPS - s if kind == 0 else s), CHIPS), core)
+
+    def ring_copy(s, kind, r, later):
+        block = weights[kind].at[r, piece(kind, origin(s, kind))]
+        return pltpu.make_async_remote_copy(
+            src_ref=block,
+            dst_ref=block,
+            send_sem=ring_send.at[s, kind, r - 1],
+            recv_sem=ring_recv.at[s + later, kind, r - 1],
+            device_id=(ring[kind], z),
+            device_id_type=MESH,
+        )
+
+    def side_copy(s, kind, owner):
+        block = weights[kind].at[pl.ds(1, 3), piece(kind, owner)]
+        return pltpu.make_async_remote_copy(
+            src_ref=block,
+            dst_ref=block,
+            send_sem=side_send.at[s, kind],
+            recv_sem=side_recv.at[s, kind],
+            device_id=(sibling, z),
+            device_id_type=MESH,
+        )
+
+    def own_copies():
+        columns = pl.ds(pl.multiple_of(z * features, features), features)
+        return (
+            pltpu.make_async_copy(value_ref.at[columns], w_value.at[0], own_sem.at[0]),
+            pltpu.make_async_copy(out_ref.at[:, columns], w_out.at[0], own_sem.at[1]),
+        )
+
+    def stage_copy(d):
+        columns = pl.ds(pl.multiple_of((d * 4 + z) * LANES, LANES), LANES)
+        return pltpu.make_async_copy(codes_ref.at[:, columns], stage.at[d], stage_sem.at[d])
+
+    def code_copy(d):
+        return pltpu.make_async_remote_copy(
+            src_ref=staged.at[d],
+            dst_ref=store_ref.at[pl.ds(pl.multiple_of(dp * rows, rows), rows)],
+            send_sem=code_send.at[d],
+            recv_sem=code_recv.at[dp],
+            device_id=(d, z),
+            device_id_type=MESH,
+        )
+
+    def code_arrival(d):
+        block = store_ref.at[pl.ds(pl.multiple_of(d * rows, rows), rows)]
+        return pltpu.make_async_remote_copy(
+            src_ref=block,
+            dst_ref=block,
+            send_sem=code_send.at[d],
+            recv_sem=code_recv.at[d],
+            device_id=(d, z),
+            device_id_type=MESH,
+        )
+
+    def sum_copy(phase, layer, k):
+        source, target, send, recv = (
+            (out1, in1, sum1_send, sum1_recv),
+            (out2, in2, sum2_send, sum2_recv),
+        )[phase]
+        return pltpu.make_async_remote_copy(
+            src_ref=source.at[layer, k],
+            dst_ref=target.at[layer, k],
+            send_sem=send.at[layer, k],
+            recv_sem=recv.at[layer, k],
+            device_id=(dp, zpair[k ^ phase]),
+            device_id_type=MESH,
+        )
+
+    for j in range(1, 4):
+        first_copy(0, j).start()
+        first_copy(1, j).start()
+        gain_copy(j).start()
+    for copy in own_copies():
+        copy.start()
+
+    def fetch(d, carry):
+        stage_copy(d).start()
+        return carry
+
+    lax.fori_loop(0, RANKS, fetch, 0)
+    gains[0] = gain_ref[z]
+    hidden_ref[...] = h_ref[...]
+
+    def scale_codes(d, carry):
+        stage_copy(d).wait()
+        staged[d] = (stage[d].astype(jnp.float32) * scale_ref[...]).astype(jnp.bfloat16)
+        return carry
+
+    lax.fori_loop(0, RANKS, scale_codes, 0)
+    store_ref[pl.ds(pl.multiple_of(dp * rows, rows), rows), :] = staged[dp]
+
+    def pass_on(s, carry):
+        for r in range(1, 4):
+            for kind in range(2):
+                ring_copy(s, kind, r, 0).wait_recv()
+
+                @pl.when(s < CHIPS - 1)
+                def _():
+                    ring_copy(s, kind, r, 1).start()
+
+        for kind in range(2):
+            side_copy(s, kind, origin(s, kind)).start()
+        return carry
+
+    lax.fori_loop(0, CHIPS, pass_on, 0)
+
+    def send_codes(j, carry):
+        code_copy(lax.rem(dp + j, RANKS)).start()
+        return carry
+
+    lax.fori_loop(1, RANKS, send_codes, 0)
+
+    def settle(s, carry):
+        for kind in range(2):
+            at = cycle_position(x, y, 1 - core)
+            owner = cycle_device(lax.rem(at + (CHIPS - s if kind == 0 else s), CHIPS), 1 - core)
+            side_copy(s, kind, owner).wait_recv()
+            side_copy(s, kind, origin(s, kind)).wait_send()
+
+            @pl.when(s < CHIPS - 1)
+            def _():
+                for r in range(1, 4):
+                    ring_copy(s, kind, r, 1).wait_send()
+
+        return carry
+
+    lax.fori_loop(0, CHIPS, settle, 0)
+    for copy in own_copies():
+        copy.wait()
+    for j in range(1, 4):
+        gain_copy(j).wait()
+
+    def layer_step(layer, carry):
+        r = lax.rem(layer - z + 4, 4)
+        gain = gains[r].astype(jnp.float32)
+        squares = jnp.zeros((rows, LANES), jnp.float32)
+        for j in range(features // LANES):
+            columns = slice(j * LANES, (j + 1) * LANES)
+            tile = hidden_ref[:, columns].astype(jnp.float32)
+            squares += tile * tile
+            normed[:, columns] = (tile * gain[j : j + 1, :]).astype(jnp.bfloat16)
+        squares = jnp.broadcast_to(jnp.sum(squares, axis=1, keepdims=True), (rows, LANES))
+        high = squares.astype(jnp.bfloat16)
+        low = (squares - high.astype(jnp.float32)).astype(jnp.bfloat16)
+        lane = lax.broadcasted_iota(jnp.int32, (rows, LANES), 1)
+        products[:, :head] = jnp.dot(normed[...], w_value[r], preferred_element_type=jnp.float32)
+        products[:, head:] = squares
+        for k in range(2):
+            part = slice(k * half, (k + 1) * half)
+            out1[layer, k, :, :head] = products[part, :head].astype(jnp.bfloat16)
+            out1[layer, k, :, head:] = jnp.where(
+                lane[part] < LANES // 2, high[part].astype(jnp.float32), low[part].astype(jnp.float32)
+            ).astype(jnp.bfloat16)
+            sum_copy(0, layer, k).start()
+
+        def arrived(buffer, k):
+            marks = buffer[layer, k, :, head:].astype(jnp.float32)
+            return buffer[layer, k, :, :head].astype(jnp.float32), marks + pltpu.roll(marks, LANES // 2, 1)
+
+        for k in range(2):
+            part = slice(k * half, (k + 1) * half)
+            sum_copy(0, layer, k).wait_recv()
+            more, marks = arrived(in1, k)
+            so_far = products[part, :head] + more
+            squares = products[part, head:] + marks
+            products[part, :head] = so_far
+            products[part, head:] = squares
+            high = squares.astype(jnp.bfloat16)
+            low = (squares - high.astype(jnp.float32)).astype(jnp.bfloat16)
+            out2[layer, k, :, :head] = so_far.astype(jnp.bfloat16)
+            out2[layer, k, :, head:] = jnp.where(
+                lane[part] < LANES // 2, high.astype(jnp.float32), low.astype(jnp.float32)
+            ).astype(jnp.bfloat16)
+            sum_copy(1, layer, k).start()
+        for k in range(2):
+            part = slice(k * half, (k + 1) * half)
+            sum_copy(1, layer, k).wait_recv()
+            more, marks = arrived(in2, k)
+            scale = lax.rsqrt((products[part, head:] + marks) * (1.0 / width) + eps)
+            for j in range(head // LANES):
+                columns = slice(j * LANES, (j + 1) * LANES)
+                values[part, columns] = ((products[part, columns] + more[:, columns]) * scale).astype(
+                    jnp.bfloat16
+                )
+        for n in range(features // 512):
+            columns = slice(n * 512, (n + 1) * 512)
+            branch = jnp.dot(values[...], w_out[r, :, columns], preferred_element_type=jnp.float32)
+            hidden_ref[:, columns] = (hidden_ref[:, columns].astype(jnp.float32) + branch).astype(
+                jnp.bfloat16
+            )
+        return carry
+
+    lax.fori_loop(0, 4, layer_step, 0)
+
+    def finish(j, carry):
+        code_arrival(lax.rem(dp + j, RANKS)).wait_recv()
+        code_copy(lax.rem(dp + j, RANKS)).wait_send()
+        return carry
+
+    lax.fori_loop(1, RANKS, finish, 0)
+    for k in range(2):
+        for layer in range(4):
+            sum_copy(0, layer, k).wait_send()
+            sum_copy(1, layer, k).wait_send()
+    for j in range(1, 4):
+        for kind in range(2):
+            first_copy(kind, j).wait_send()
+
+
+def layers(hidden, value_weight, folded_out, gain, codes, scales):
+    rows, features = hidden.shape
+    head = value_weight.shape[1]
+    half = rows // 2
+    vmem = pl.BlockSpec(memory_space=pltpu.VMEM)
+    anywhere = pl.BlockSpec(memory_space=pl.ANY)
+    dma = pltpu.SemaphoreType.DMA
+    message = (4, 2, half, head + LANES)
+    return pl.pallas_call(
+        functools.partial(layers_kernel, 1e-5),
+        out_shape=(
+            jax.ShapeDtypeStruct((rows, features), jnp.bfloat16),
+            jax.ShapeDtypeStruct((rows * RANKS, LANES), jnp.bfloat16),
+        ),
+        in_specs=[vmem, anywhere, anywhere, vmem, anywhere, vmem],
+        out_specs=(vmem, vmem),
+        scratch_shapes=[
+            pltpu.VMEM((4, features, head), jnp.bfloat16),
+            pltpu.VMEM((4, head, features), jnp.bfloat16),
+            pltpu.VMEM((4, features // LANES, LANES), jnp.bfloat16),
+            pltpu.VMEM((rows, head + LANES), jnp.float32),
+            pltpu.VMEM((rows, features), jnp.bfloat16),
+            pltpu.VMEM((rows, head), jnp.bfloat16),
+            pltpu.VMEM(message, jnp.bfloat16),
+            pltpu.VMEM(message, jnp.bfloat16),
+            pltpu.VMEM(message, jnp.bfloat16),
+            pltpu.VMEM(message, jnp.bfloat16),
+            pltpu.VMEM((RANKS, rows, LANES), jnp.bfloat16),
+            pltpu.VMEM((RANKS, rows, LANES), jnp.bfloat16),
+            dma((2,)),
+            dma((2, 3)),
+            dma((CHIPS, 2, 3)),
+            dma((CHIPS, 2, 3)),
+            dma((CHIPS, 2)),
+            dma((CHIPS, 2)),
+            dma((3,)),
+            dma((3,)),
+            dma((4, 2)),
+            dma((4, 2)),
+            dma((4, 2)),
+            dma((4, 2)),
+            dma((RANKS,)),
+            dma((RANKS,)),
+            dma((RANKS,)),
+        ],
+        compiler_params=pltpu.CompilerParams(
+            collective_id=1, has_side_effects=True, vmem_limit_bytes=40 * 1024 * 1024
+        ),
+    )(hidden, value_weight, folded_out, gain, codes, scales)
+
+
 def wide_kernel(
     inv_root,
     h_ref,
     proj_ref,
-    target_ref,
+    store_ref,
+    perm_ref,
     grad_ref,
     loss_ref,
     held,
@@ -47,6 +412,9 @@
     out2,
     in2,
     rows_g,
+    store,
+    aim,
+    losses,
     own_sem,
     ring_send,
     ring_recv,
@@ -60,6 +428,8 @@
     rows1_recv,
     rows2_send,
     rows2_recv,
+    loss_send,
+    loss_recv,
 ):
     dp = lax.axis_index("dp")
     z = lax.axis_index("pipe")
@@ -77,10 +447,24 @@
     zpair = (za, zb)
     ring = (after, before)
 
+    sizes = (4, SIDE, 2 * SIDE)
+    spots = (z, y, 2 * x + core)
+
+    def peer(group, j):
+        spot = lax.rem(spots[group] + j, sizes[group])
+        if group == 0:
+            return dp, spot
+        if group == 1:
+            return (x * SIDE + spot) * 2 + core, z
+        return ((spot // 2) * SIDE + y) * 2 + lax.rem(spot, 2), z
+
     barrier = pltpu.get_barrier_semaphore()
-    for device in ((after, z), (before, z), (sibling, z), (dp, za), (dp, zb)):
+    for device in ((after, z), (before, z)):
         pl.semaphore_signal(barrier, inc=1, device_id=device, device_id_type=MESH)
-    pl.semaphore_wait(barrier, 5)
+    for group in range(3):
+        for j in range(1, sizes[group]):
+            pl.semaphore_signal(barrier, inc=1, device_id=peer(group, j), device_id_type=MESH)
+    pl.semaphore_wait(barrier, 2 + sum(sizes) - 3)
 
     mine = pl.multiple_of(core * 2 * part, 2 * part)
     theirs = pl.multiple_of((1 - core) * 2 * part, 2 * part)
@@ -162,6 +546,30 @@
             device_id_type=MESH,
         )
 
+    def loss_copy(group, j, arrival):
+        spot = lax.rem(spots[group] + j, sizes[group]) if arrival else spots[group]
+        return pltpu.make_async_remote_copy(
+            src_ref=losses.at[group, spot],
+            dst_ref=losses.at[group, spot],
+            send_sem=loss_send.at[group, j],
+            recv_sem=loss_recv.at[group, spot],
+            device_id=peer(group, j),
+            device_id_type=MESH,
+        )
+
+    def loss_out(group):
+        losses[group, spots[group]] = loss_ref[...]
+        for j in range(1, sizes[group]):
+            loss_copy(group, j, False).start()
+
+    def loss_in(group):
+        for j in range(1, sizes[group]):
+            loss_copy(group, j, True).wait_recv()
+        loss_ref[...] = functools.reduce(
+            jnp.add, [losses[group, spot] for spot in range(sizes[group])]
+        )
+
+    store[...] = store_ref[...].astype(jnp.float32)
     loss_ref[...] = jnp.zeros_like(loss_ref)
     total[...] = jnp.zeros_like(total)
     own_copy().start()
@@ -208,10 +616,20 @@
                 token = pl.multiple_of((origin * 2 + way) * part, part)
                 rows = pl.ds(chunk * part, part)
                 inside = pl.ds((chunk % 2) * part, part)
+
+                def seek(group, carry):
+                    for j in range(8):
+                        at_row = group * 8 + j
+                        aim[pl.ds(chunk * part + at_row, 1), :] = store[
+                            pl.ds(perm_ref[token + at_row], 1), :
+                        ]
+                    return carry
+
+                lax.fori_loop(0, part // 8, seek, 0)
                 diff = (
                     y_keep[slot, rows, :]
                     + in2[s, chunk // 2, inside, :].astype(jnp.float32)
-                    - target_ref[pl.ds(token, part), :]
+                    - aim[rows, :]
                 )
                 rows_g[s, z, rows, :] = (diff * inv_root).astype(jnp.bfloat16)
                 loss_ref[...] += jnp.sum((diff * diff).reshape(part // 8, 8, diff.shape[1]), axis=0)
@@ -225,6 +643,15 @@
                 rows1_copy(s, k, zpair[k]).wait_recv()
             for k in range(2):
                 rows2_copy(s, k, zpair[1 - k]).start()
+
+        @pl.when(i == steps + 2)
+        def _():
+            loss_out(0)
+
+        @pl.when(i == steps + 3)
+        def _():
+            loss_in(0)
+            loss_out(1)
 
         @pl.when(i < steps)
         def _():
@@ -259,6 +686,8 @@
         return carry
 
     lax.fori_loop(0, steps + 4, body, 0)
+    loss_in(1)
+    loss_out(2)
 
     def finish(s, carry):
         @pl.when(s < steps - 1)
@@ -275,10 +704,14 @@
         return carry
 
     lax.fori_loop(0, steps, finish, 0)
+    loss_in(2)
+    for group in range(3):
+        for j in range(1, sizes[group]):
+            loss_copy(group, j, False).wait_send()
     grad_ref[...] = total[...].astype(jnp.bfloat16)
 
 
-def wide(hidden, proj, target, inv_root):
+def wide(hidden, proj, store, perm, inv_root):
     rows, features = hidden.shape
     columns = proj.shape[1]
     quarter = columns // 4
@@ -292,7 +725,7 @@
             jax.ShapeDtypeStruct((features, columns), jnp.bfloat16),
             jax.ShapeDtypeStruct((8, quarter), jnp.float32),
         ),
-        in_specs=[vmem] * 3,
+        in_specs=[vmem, vmem, vmem, pl.BlockSpec(memory_space=pltpu.SMEM)],
         out_specs=(vmem, vmem),
         scratch_shapes=[
             pltpu.VMEM((CHIPS, block, features), jnp.bfloat16),
@@ -304,58 +737,34 @@
             pltpu.VMEM((CHIPS, 2, half, quarter), jnp.bfloat16),
             pltpu.VMEM((CHIPS, 2, half, quarter), jnp.bfloat16),
             pltpu.VMEM((CHIPS, 4, block, quarter), jnp.bfloat16),
+            pltpu.VMEM(store.shape, jnp.float32),
+            pltpu.VMEM((block, quarter), jnp.float32),
+            pltpu.VMEM((3, 2 * SIDE, 8, quarter), jnp.float32),
             pltpu.SemaphoreType.DMA,
         ]
-        + [pairs] * 12,
+        + [pairs] * 12
+        + [pltpu.SemaphoreType.DMA((3, 2 * SIDE))] * 2,
         compiler_params=pltpu.CompilerParams(
             collective_id=0, has_side_effects=True, vmem_limit_bytes=56 * 1024 * 1024
         ),
-    )(hidden, proj, target)
+    )(hidden, proj, store, perm)
 
 
 def shards(
     student_in, value_weight, folded_out, norm_gain, proj, teacher_codes, teacher_scales, perm
 ):
     sections = lax.axis_size("pipe")
-    section = lax.axis_index("pipe")
     n_ranks = lax.axis_size("dp")
-    rank = lax.axis_index("dp")
     rows, features = student_in.shape
-    width = features * sections
-    head = value_weight.shape[2]
     tokens = rows * n_ranks
     columns = proj.shape[1]
     total_cols = columns * n_ranks
 
-    scaled = value_weight[0].astype(jnp.float32) * norm_gain[0].astype(jnp.float32)[:, None]
-    w_value = scaled.astype(jnp.bfloat16).reshape(sections, n_ranks, features // n_ranks, head)
-    w_value = lax.dynamic_index_in_dim(w_value, rank, 1, keepdims=False)
-    w_value = lax.all_to_all(w_value, "pipe", split_axis=0, concat_axis=0, tiled=True)
-    w_value = lax.all_gather(w_value, "dp", axis=1, tiled=True)
-    w_out = lax.dynamic_slice_in_dim(folded_out[0], rank * (head // n_ranks), head // n_ranks, 0)
-    w_out = w_out.reshape(head // n_ranks, sections, features).transpose(1, 0, 2)
-    w_out = lax.all_to_all(w_out, "pipe", split_axis=0, concat_axis=0, tiled=True)
-    w_out = lax.all_gather(w_out, "dp", axis=1, tiled=True)
-
-    codes = teacher_codes.reshape(rows, n_ranks, sections, columns // sections)
-    codes = lax.dynamic_index_in_dim(codes, section, 2, keepdims=False)
-    codes = lax.all_to_all(codes, "dp", split_axis=1, concat_axis=0, tiled=True).reshape(tokens, -1)
-    scales = lax.all_gather(teacher_scales, "dp", axis=0, tiled=True)
-    target = codes[perm].astype(jnp.float32) * scales[perm].astype(jnp.float32)[:, None]
-
-    hidden = student_in
-    for layer in range(sections):
-        wide_rows = hidden.astype(jnp.float32)
-        squares = jnp.sum(wide_rows * wide_rows, axis=1, keepdims=True)
-        products = jnp.dot(hidden, w_value[layer], preferred_element_type=jnp.float32)
-        both = lax.psum(jnp.concatenate([products, jnp.broadcast_to(squares, (rows, 128))], axis=1), "pipe")
-        scale = lax.rsqrt(both[:, head : head + 1] / width + 1e-05)
-        values = (both[:, :head] * scale).astype(jnp.bfloat16)
-        branch = jnp.dot(values, w_out[layer], preferred_element_type=jnp.float32)
-        hidden = (wide_rows + branch).astype(jnp.bfloat16)
-
-    grad_proj, squared = wide(hidden, proj, target, 1.0 / math.sqrt(tokens))
-    loss = 0.5 * lax.psum(jnp.sum(squared), ("dp", "pipe")) / (tokens * total_cols)
+    gain = norm_gain.reshape(sections, features // LANES, LANES)
+    scales = jnp.broadcast_to(teacher_scales.astype(jnp.float32)[:, None], (rows, LANES))
+    hidden, store = layers(student_in, value_weight[0], folded_out[0], gain, teacher_codes, scales)
+    grad_proj, squared = wide(hidden, proj, store, perm, 1.0 / math.sqrt(tokens))
+    loss = 0.5 * jnp.sum(squared) / (tokens * total_cols)
     return (grad_proj, loss)
 
 

time: 541 us -> 258 us (0.48)
  waiting for transfers between devices: 165 us -> 0 us
  Pallas kernels: 119 us -> 245 us
  blocking collectives: 107 us -> 0 us
  local copies, waits for them, and re-layouts: 85.7 us -> 8.77 us
  matrix products: 25.6 us -> 0 us
  between operations: 16.1 us -> 2.45 us
  starting transfers between devices: 10.2 us -> 0 us
  other arithmetic: 11.2 us -> 2.14 us
    pallas_call x0 -> x1, Pallas kernels: none -> 113 us  [layers(): pl.pallas_call(functools.partial(layers_kernel, 1e-05), out_shape=(jax.Sh...]
    all_gather x2 -> x0, waiting for transfers between devices: 95.4 us -> none  [the longest x1 51.5 us: shards(): w_out = lax.all_gather(w_out, 'dp', axis=1, tiled=True)]
    psum x4 -> x0, waiting for transfers between devices: 69.7 us -> none  [shards(): lax.psum(jnp.concatenate([products, jnp.broadcast_to(squares, (rows, 128)...]
    psum x1 -> x0, blocking collectives: 64.3 us -> none  [shards(): lax.psum(jnp.sum(squared), ('dp', 'pipe'))]
    gather x2 -> x0, local copies, waits for them, and re-layouts: 37.8 us -> none  [the longest x1 25.6 us: shards(): scales[perm].astype(jnp.float32)[:, None]]
    slice x1 -> x0, local copies, waits for them, and re-layouts: 27.9 us -> none  [shards(): branch = jnp.dot(values, w_out[layer], preferred_element_type=jnp.float32)]
    dot_general x8 -> x0, matrix products: 25.6 us -> none  [the longest x4 15.7 us: shards(): branch = jnp.dot(values, w_out[layer], preferred_element_type=jnp.float32)]
    all_gather x1 -> x0, blocking collectives: 23.3 us -> none  [shards(): scales = lax.all_gather(teacher_scales, 'dp', axis=0, tiled=True)]
  transfers between devices with their start and end apart: 7 -> 0, of which waited for: 5 -> 0; matrix products, arithmetic and copies ran while one was open for 18% -> 0% of each run, Pallas kernels for 0% -> 0%
where the time goes in v2:
time: 258 us
  Pallas kernels  245 us (95%)
  local copies, waits for them, and re-layouts  8.77 us (3%)
    pallas_call x1, Pallas kernels, wide(): pl.pallas_call(functools.partial(wide_kernel, inv_root), out_shape=(jax.S...  132 us
    pallas_call x1, Pallas kernels, layers(): pl.pallas_call(functools.partial(layers_kernel, 1e-05), out_shape=(jax.Sh...  113 us
    unnamed x9, local copies, waits for them, and re-layouts  8.04 us

profile of v2, /device:TPU:1, one launch (start us, length us, event | category | flops | bytes accessed | tf_op | source)
XLA Modules:
  0.0 258.0 jit_solution(11958034957906419309)
XLA Ops:
  0.6 0.8 reduce
  1.5 0.7 broadcast_in_dim.2.scale_ref
  2.2 0.0 copy-start
  2.2 2.2 copy-done
  4.4 0.0 copy-start.2
  4.4 1.0 copy-done.2
  5.5 113.1 %shard_map.95 = (bf16[128,2048]{1,0:T(8,128)(2,1)S(1)}, bf16[4096,128]{1,0:T(8,128)(2,1)S(1)}) custom-call(bf16[128,2048]{1,0:T(8,128)(2,1)S(1)} %copy-done.2, bf16[8192,512]{1,0:T(8,128)(2,1)} %bitcast.4, bf16[512,8192]{1,0:T(8,128)(2,1)} %bitcast.5, bf16[4,16,128]{2,1,0:T(8,128)(2,1)S(1)} %bitcast.3, bf16[128,16384]{1,0:T(8,128)(2,1)S(1)} %copy-done, ...), custom_call_target="tpu_custom_call" | custom-call | tf_op jit(solution)/shard_map/pallas_call | solution.py:355
  118.5 0.0 copy-start.1
  118.6 1.0 copy-done.1
  119.5 0.0 copy-start.3
  119.5 0.8 copy-done.3
  120.3 131.5 %shard_map.96 = (bf16[2048,512]{1,0:T(8,128)(2,1)}, f32[8,128]{1,0:T(8,128)}) custom-call(bf16[128,2048]{1,0:T(8,128)(2,1)} %copy-done.3, bf16[2048,512]{1,0:T(8,128)(2,1)} %proj_ref.1, bf16[4096,128]{1,0:T(8,128)(2,1)} %copy-done.1, s32[4096]{0:T(1024)} %perm_ref.1), custom_call_target="tpu_custom_call" | custom-call | tf_op jit(solution)/shard_map/pallas_call | solution.py:722
  251.8 1.3 reduce_sum.9
  253.8 3.0 %copy.11 = bf16[2048,512]{1,0:T(8,128)(2,1)} copy(bf16[2048,512]{1,0:T(8,128)(2,1)} %get-tuple-element.12) | data formatting | bytes 4194304
Async XLA Ops:
  2.2 2.2 copy-start
  4.4 1.0 copy-start.2
  118.5 1.0 copy-start.1
  119.5 0.8 copy-start.3

commit v3 on v2

--- a/solution.py
+++ b/solution.py
@@ -57,8 +57,11 @@
     staged,
     own_sem,
     first_send,
-    ring_send,
-    ring_recv,
+    first_recv,
+    near_send,
+    near_recv,
+    far_send,
+    far_recv,
     side_send,
     side_recv,
     gain_send,
@@ -74,17 +77,12 @@
     dp = lax.axis_index("dp")
     z = lax.axis_index("pipe")
     x, y, core = place(dp)
-    here = cycle_position(x, y, core)
-    after = cycle_device(lax.rem(here + 1, CHIPS), core)
-    before = cycle_device(lax.rem(here + CHIPS - 1, CHIPS), core)
     sibling = dp + 1 - 2 * core
     zpair = (z + 1 - 2 * lax.rem(z, 2), 3 - z)
-    ring = (after, before)
     rows, features = h_ref.shape
-    head = value_ref.shape[1]
+    head = value_ref.shape[-1]
     half = rows // 2
     weights = (w_value, w_out)
-    depth = (features // RANKS, head // RANKS)
     width = 4 * features
 
     barrier = pltpu.get_barrier_semaphore()
@@ -102,22 +100,71 @@
         )
     pl.semaphore_wait(barrier, RANKS + 2)
 
-    def piece(kind, owner):
-        return pl.ds(pl.multiple_of(owner * depth[kind], depth[kind]), depth[kind])
-
     def first_copy(kind, j):
         to = lax.rem(z + j, 4)
         if kind == 0:
-            start = pl.multiple_of(to * features + dp * depth[0], depth[0])
-            source = value_ref.at[pl.ds(start, depth[0])]
+            source = value_ref.at[to, x, y, core]
         else:
-            source = out_ref.at[piece(1, dp), pl.ds(pl.multiple_of(to * features, features), features)]
+            source = out_ref.at[x, y, core, :, pl.ds(pl.multiple_of(to * features, features), features)]
         return pltpu.make_async_remote_copy(
             src_ref=source,
-            dst_ref=weights[kind].at[4 - j, piece(kind, dp)],
+            dst_ref=weights[kind].at[4 - j, x, y, core],
             send_sem=first_send.at[kind, j - 1],
-            recv_sem=ring_recv.at[0, kind, 3 - j],
+            recv_sem=first_recv.at[kind, 3 - j],
             device_id=(dp, to),
+            device_id_type=MESH,
+        )
+
+    def first_arrival(kind, r):
+        block = weights[kind].at[r, x, y, core]
+        return pltpu.make_async_remote_copy(
+            src_ref=block,
+            dst_ref=block,
+            send_sem=first_send.at[kind, r - 1],
+            recv_sem=first_recv.at[kind, r - 1],
+            device_id=(dp, lax.rem(z + r, 4)),
+            device_id_type=MESH,
+        )
+
+    spot = (x, y)
+
+    def near_copy(kind, r, j, arrival):
+        there = lax.rem(spot[kind] + j, SIDE)
+        at = there if arrival else spot[kind]
+        block = w_value.at[r, at, y, core] if kind == 0 else w_out.at[r, x, at, core]
+        chip = there * SIDE + y if kind == 0 else x * SIDE + there
+        return pltpu.make_async_remote_copy(
+            src_ref=block,
+            dst_ref=block,
+            send_sem=near_send.at[kind, r - 1, j],
+            recv_sem=near_recv.at[kind, r - 1, at],
+            device_id=(chip * 2 + core, z),
+            device_id_type=MESH,
+        )
+
+    def far_copy(kind, r, j, arrival):
+        there = lax.rem(spot[1 - kind] + j, SIDE)
+        at = there if arrival else spot[1 - kind]
+        block = w_value.at[r, :, at, core] if kind == 0 else w_out.at[r, at, :, core]
+        chip = there * SIDE + y if kind == 1 else x * SIDE + there
+        return pltpu.make_async_remote_copy(
+            src_ref=block,
+            dst_ref=block,
+            send_sem=far_send.at[kind, r - 1, j],
+            recv_sem=far_recv.at[kind, r - 1, at],
+            device_id=(chip * 2 + core, z),
+            device_id_type=MESH,
+        )
+
+    def side_copy(kind, r, j, owner):
+        at = lax.rem(spot[1 - kind] + j, SIDE)
+        block = w_value.at[r, :, at, owner] if kind == 0 else w_out.at[r, at, :, owner]
+        return pltpu.make_async_remote_copy(
+            src_ref=block,
+            dst_ref=block,
+            send_sem=side_send.at[kind, r - 1, at],
+            recv_sem=side_recv.at[kind, r - 1, at],
+            device_id=(sibling, z),
             device_id_type=MESH,
         )
 
@@ -132,36 +179,11 @@
             device_id_type=MESH,
         )
 
-    def origin(s, kind):
-        return cycle_device(lax.rem(here + (CHIPS - s if kind == 0 else s), CHIPS), core)
-
-    def ring_copy(s, kind, r, later):
-        block = weights[kind].at[r, piece(kind, origin(s, kind))]
-        return pltpu.make_async_remote_copy(
-            src_ref=block,
-            dst_ref=block,
-            send_sem=ring_send.at[s, kind, r - 1],
-            recv_sem=ring_recv.at[s + later, kind, r - 1],
-            device_id=(ring[kind], z),
-            device_id_type=MESH,
-        )
-
-    def side_copy(s, kind, owner):
-        block = weights[kind].at[pl.ds(1, 3), piece(kind, owner)]
-        return pltpu.make_async_remote_copy(
-            src_ref=block,
-            dst_ref=block,
-            send_sem=side_send.at[s, kind],
-            recv_sem=side_recv.at[s, kind],
-            device_id=(sibling, z),
-            device_id_type=MESH,
-        )
-
     def own_copies():
         columns = pl.ds(pl.multiple_of(z * features, features), features)
         return (
-            pltpu.make_async_copy(value_ref.at[columns], w_value.at[0], own_sem.at[0]),
-            pltpu.make_async_copy(out_ref.at[:, columns], w_out.at[0], own_sem.at[1]),
+            pltpu.make_async_copy(value_ref.at[z], w_value.at[0], own_sem.at[0]),
+            pltpu.make_async_copy(out_ref.at[:, :, :, :, columns], w_out.at[0], own_sem.at[1]),
         )
 
     def stage_copy(d):
@@ -226,49 +248,67 @@
     lax.fori_loop(0, RANKS, scale_codes, 0)
     store_ref[pl.ds(pl.multiple_of(dp * rows, rows), rows), :] = staged[dp]
 
-    def pass_on(s, carry):
-        for r in range(1, 4):
+    def turn(k):
+        layer = k + jnp.where(k >= z, 1, 0)
+        return lax.rem(layer - z + 4, 4)
+
+    def spread_near(k, carry):
+        r = turn(k)
+        for kind in range(2):
+            first_arrival(kind, r).wait_recv()
+            for j in (1, 3, 2):
+                near_copy(kind, r, j, False).start()
+        return carry
+
+    def spread_far(k):
+        r = turn(k)
+        for kind in range(2):
+            for j in (1, 3, 2):
+                near_copy(kind, r, j, True).wait_recv()
+            for j in (1, 3, 2):
+                far_copy(kind, r, j, False).start()
+        for kind in range(2):
+            side_copy(kind, r, 0, core).start()
+
+    def settle(r, order):
+        for j in order:
             for kind in range(2):
-                ring_copy(s, kind, r, 0).wait_recv()
-
-                @pl.when(s < CHIPS - 1)
-                def _():
-                    ring_copy(s, kind, r, 1).start()
-
-        for kind in range(2):
-            side_copy(s, kind, origin(s, kind)).start()
-        return carry
-
-    lax.fori_loop(0, CHIPS, pass_on, 0)
-
-    def send_codes(j, carry):
-        code_copy(lax.rem(dp + j, RANKS)).start()
-        return carry
-
-    lax.fori_loop(1, RANKS, send_codes, 0)
-
-    def settle(s, carry):
-        for kind in range(2):
-            at = cycle_position(x, y, 1 - core)
-            owner = cycle_device(lax.rem(at + (CHIPS - s if kind == 0 else s), CHIPS), 1 - core)
-            side_copy(s, kind, owner).wait_recv()
-            side_copy(s, kind, origin(s, kind)).wait_send()
-
-            @pl.when(s < CHIPS - 1)
-            def _():
-                for r in range(1, 4):
-                    ring_copy(s, kind, r, 1).wait_send()
-
-        return carry
-
-    lax.fori_loop(0, CHIPS, settle, 0)
+                far_copy(kind, r, j, True).wait_recv()
+                side_copy(kind, r, j, core).start()
+
+    lax.fori_loop(0, 3, spread_near, 0)
+    spread_far(0)
     for copy in own_copies():
         copy.wait()
     for j in range(1, 4):
         gain_copy(j).wait()
 
+    def send_codes(j, carry):
+        code_copy(lax.rem(dp + j, RANKS)).start()
+        return carry
+
     def layer_step(layer, carry):
         r = lax.rem(layer - z + 4, 4)
+
+        @pl.when(layer != z)
+        def _():
+            settle(r, (1,))
+
+        @pl.when(layer < 2)
+        def _():
+            spread_far(layer + 1)
+
+        @pl.when(layer != z)
+        def _():
+            settle(r, (3, 2))
+            for kind in range(2):
+                for j in range(SIDE):
+                    side_copy(kind, r, j, 1 - core).wait_recv()
+
+            @pl.when(layer == 3 - jnp.where(z == 3, 1, 0))
+            def _():
+                lax.fori_loop(1, RANKS, send_codes, 0)
+
         gain = gains[r].astype(jnp.float32)
         squares = jnp.zeros((rows, LANES), jnp.float32)
         for j in range(features // LANES):
@@ -280,7 +320,9 @@
         high = squares.astype(jnp.bfloat16)
         low = (squares - high.astype(jnp.float32)).astype(jnp.bfloat16)
         lane = lax.broadcasted_iota(jnp.int32, (rows, LANES), 1)
-        products[:, :head] = jnp.dot(normed[...], w_value[r], preferred_element_type=jnp.float32)
+        products[:, :head] = jnp.dot(
+            normed[...], w_value[r].reshape(features, head), preferred_element_type=jnp.float32
+        )
         products[:, head:] = squares
         for k in range(2):
             part = slice(k * half, (k + 1) * half)
@@ -321,7 +363,11 @@
                 )
         for n in range(features // 512):
             columns = slice(n * 512, (n + 1) * 512)
-            branch = jnp.dot(values[...], w_out[r, :, columns], preferred_element_type=jnp.float32)
+            branch = jnp.dot(
+                values[...],
+                w_out[r, :, :, :, :, columns].reshape(head, 512),
+                preferred_element_type=jnp.float32,
+            )
             hidden_ref[:, columns] = (hidden_ref[:, columns].astype(jnp.float32) + branch).astype(
                 jnp.bfloat16
             )
@@ -342,12 +388,22 @@
     for j in range(1, 4):
         for kind in range(2):
             first_copy(kind, j).wait_send()
+            for r in range(1, 4):
+                near_copy(kind, r, j, False).wait_send()
+                far_copy(kind, r, j, False).wait_send()
+    for kind in range(2):
+        for r in range(1, 4):
+            for j in range(SIDE):
+                side_copy(kind, r, j, core).wait_send()
 
 
 def layers(hidden, value_weight, folded_out, gain, codes, scales):
     rows, features = hidden.shape
     head = value_weight.shape[1]
     half = rows // 2
+    grid = (4, SIDE, SIDE, 2)
+    value_weight = value_weight.reshape(*grid, features // RANKS, head)
+    folded_out = folded_out.reshape(*grid[1:], head // RANKS, 4 * features)
     vmem = pl.BlockSpec(memory_space=pltpu.VMEM)
     anywhere = pl.BlockSpec(memory_space=pl.ANY)
     dma = pltpu.SemaphoreType.DMA
@@ -361,8 +417,8 @@
         in_specs=[vmem, anywhere, anywhere, vmem, anywhere, vmem],
         out_specs=(vmem, vmem),
         scratch_shapes=[
-            pltpu.VMEM((4, features, head), jnp.bfloat16),
-            pltpu.VMEM((4, head, features), jnp.bfloat16),
+            pltpu.VMEM((*grid, features // RANKS, head), jnp.bfloat16),
+            pltpu.VMEM((*grid, head // RANKS, features), jnp.bfloat16),
             pltpu.VMEM((4, features // LANES, LANES), jnp.bfloat16),
             pltpu.VMEM((rows, head + LANES), jnp.float32),
             pltpu.VMEM((rows, features), jnp.bfloat16),
@@ -375,10 +431,13 @@
             pltpu.VMEM((RANKS, rows, LANES), jnp.bfloat16),
             dma((2,)),
             dma((2, 3)),
-            dma((CHIPS, 2, 3)),
-            dma((CHIPS, 2, 3)),
-            dma((CHIPS, 2)),
-            dma((CHIPS, 2)),
+            dma((2, 3)),
+            dma((2, 3, SIDE)),
+            dma((2, 3, SIDE)),
+            dma((2, 3, SIDE)),
+            dma((2, 3, SIDE)),
+            dma((2, 3, SIDE)),
+            dma((2, 3, SIDE)),
             dma((3,)),
             dma((3,)),
             dma((4, 2)),
@@ -472,35 +531,25 @@
     def own_copy():
         return pltpu.make_async_copy(h_ref, held.at[0, pl.ds(mine, 2 * part)], own_sem)
 
-    def ring_copy(s, way):
-        rows = pl.ds(pl.multiple_of(mine + way * part, part), part)
+    def ring_copy(s, way, sub, later):
+        start = mine + way * part + sub * (part // 2)
+        rows = pl.ds(pl.multiple_of(start, part // 2), part // 2)
         return pltpu.make_async_remote_copy(
             src_ref=held.at[s, rows],
-            dst_ref=held.at[s + 1, rows],
-            send_sem=ring_send.at[s, way],
-            recv_sem=ring_recv.at[s + 1, way],
+            dst_ref=held.at[s + later, rows],
+            send_sem=ring_send.at[s, way, sub],
+            recv_sem=ring_recv.at[s + later, way, sub],
             device_id=(ring[way], z),
             device_id_type=MESH,
         )
 
-    def ring_arrival(s, way):
-        rows = pl.ds(pl.multiple_of(mine + way * part, part), part)
+    def side_copy(s, start):
+        rows = pl.ds(start, 2 * part)
         return pltpu.make_async_remote_copy(
             src_ref=held.at[s, rows],
             dst_ref=held.at[s, rows],
-            send_sem=ring_send.at[s, way],
-            recv_sem=ring_recv.at[s, way],
-            device_id=(ring[way], z),
-            device_id_type=MESH,
-        )
-
-    def side_copy(s, way, start):
-        rows = pl.ds(pl.multiple_of(start + way * part, part), part)
-        return pltpu.make_async_remote_copy(
-            src_ref=held.at[s, rows],
-            dst_ref=held.at[s, rows],
-            send_sem=side_send.at[s, way],
-            recv_sem=side_recv.at[s, way],
+            send_sem=side_send.at[s],
+            recv_sem=side_recv.at[s],
             device_id=(sibling, z),
             device_id_type=MESH,
         )
@@ -575,25 +624,41 @@
     own_copy().start()
     own_copy().wait()
 
+    def pass_on(i, sub):
+        @pl.when(jnp.logical_and(i > 0, i < steps))
+        def _():
+            for way in range(2):
+                ring_copy(i, way, sub, 0).wait_recv()
+
+        @pl.when(i < steps - 1)
+        def _():
+            for way in range(2):
+                ring_copy(i, way, sub, 1).start()
+
     def body(i, carry):
-        @pl.when(i < steps)
-        def _():
-            @pl.when(i > 0)
-            def _():
-                for way in range(2):
-                    ring_arrival(i, way).wait_recv()
-
-            @pl.when(i < steps - 1)
-            def _():
-                for way in range(2):
-                    ring_copy(i, way).start()
-
-            for way in range(2):
-                side_copy(i, way, mine).start()
+        pass_on(i, 0)
 
         @pl.when(jnp.logical_and(i >= 1, i < steps + 1))
         def _():
             s = i - 1
+            slot = lax.rem(s, 2)
+            side_copy(s, theirs).wait_recv()
+            for n in range(2):
+                part_y = jnp.dot(
+                    held[s], proj_ref[:, n * 256 : (n + 1) * 256], preferred_element_type=jnp.float32
+                )
+                y_own[slot, 2 * n] = part_y[:, :128]
+                y_own[slot, 2 * n + 1] = part_y[:, 128:]
+            for k in range(2):
+                rows = pl.ds(k * half, half)
+                other = 3 - zpair[k] if k == 0 else zpair[k] + 1 - 2 * lax.rem(zpair[k], 2)
+                out1[s, k, 0] = y_own[slot, zpair[k], rows, :].astype(jnp.bfloat16)
+                out1[s, k, 1] = y_own[slot, other, rows, :].astype(jnp.bfloat16)
+                sum1_copy(s, k).start()
+
+        @pl.when(jnp.logical_and(i >= 2, i < steps + 2))
+        def _():
+            s = i - 2
             slot = lax.rem(s, 2)
             for k in range(2):
                 rows = pl.ds(k * half, half)
@@ -603,9 +668,15 @@
                 sum2_copy(s, k).start()
                 y_keep[slot, rows, :] = y_own[slot, z, rows, :] + in1[s, k, 0].astype(jnp.float32)
 
-        @pl.when(jnp.logical_and(i >= 2, i < steps + 2))
-        def _():
-            s = i - 2
+        pass_on(i, 1)
+
+        @pl.when(i < steps)
+        def _():
+            side_copy(i, mine).start()
+
+        @pl.when(jnp.logical_and(i >= 3, i < steps + 3))
+        def _():
+            s = i - 3
             slot = lax.rem(s, 2)
             for k in range(2):
                 sum2_copy(s, k).wait_recv()
@@ -636,44 +707,26 @@
             for k in range(2):
                 rows1_copy(s, k, z).start()
 
-        @pl.when(jnp.logical_and(i >= 3, i < steps + 3))
-        def _():
-            s = i - 3
+        @pl.when(jnp.logical_and(i >= 4, i < steps + 4))
+        def _():
+            s = i - 4
             for k in range(2):
                 rows1_copy(s, k, zpair[k]).wait_recv()
             for k in range(2):
                 rows2_copy(s, k, zpair[1 - k]).start()
 
-        @pl.when(i == steps + 2)
+        @pl.when(i == steps + 3)
         def _():
             loss_out(0)
 
-        @pl.when(i == steps + 3)
+        @pl.when(i == steps + 4)
         def _():
             loss_in(0)
             loss_out(1)
 
-        @pl.when(i < steps)
-        def _():
-            slot = lax.rem(i, 2)
-            for way in range(2):
-                side_copy(i, way, theirs).wait_recv()
-            for n in range(2):
-                part_y = jnp.dot(
-                    held[i], proj_ref[:, n * 256 : (n + 1) * 256], preferred_element_type=jnp.float32
-                )
-                y_own[slot, 2 * n] = part_y[:, :128]
-                y_own[slot, 2 * n + 1] = part_y[:, 128:]
-            for k in range(2):
-                rows = pl.ds(k * half, half)
-                other = 3 - zpair[k] if k == 0 else zpair[k] + 1 - 2 * lax.rem(zpair[k], 2)
-                out1[i, k, 0] = y_own[slot, zpair[k], rows, :].astype(jnp.bfloat16)
-                out1[i, k, 1] = y_own[slot, other, rows, :].astype(jnp.bfloat16)
-                sum1_copy(i, k).start()
-
-        @pl.when(i >= 4)
-        def _():
-            s = i - 4
+        @pl.when(i >= 5)
+        def _():
+            s = i - 5
             for k in range(2):
                 rows2_copy(s, k, 3 - zpair[k] if k == 0 else zpair[k] + 1 - 2 * lax.rem(zpair[k], 2)).wait_recv()
             rows = jnp.concatenate([rows_g[s, q] for q in range(4)], axis=1)
@@ -685,7 +738,7 @@
 
         return carry
 
-    lax.fori_loop(0, steps + 4, body, 0)
+    lax.fori_loop(0, steps + 5, body, 0)
     loss_in(1)
     loss_out(2)
 
@@ -693,10 +746,11 @@
         @pl.when(s < steps - 1)
         def _():
             for way in range(2):
-                ring_copy(s, way).wait_send()
-
+                for sub in range(2):
+                    ring_copy(s, way, sub, 1).wait_send()
+
+        side_copy(s, mine).wait_send()
         for k in range(2):
-            side_copy(s, k, mine).wait_send()
             sum1_copy(s, k).wait_send()
             sum2_copy(s, k).wait_send()
             rows1_copy(s, k, z).wait_send()
@@ -742,7 +796,9 @@
             pltpu.VMEM((3, 2 * SIDE, 8, quarter), jnp.float32),
             pltpu.SemaphoreType.DMA,
         ]
-        + [pairs] * 12
+        + [pltpu.SemaphoreType.DMA((CHIPS, 2, 2))] * 2
+        + [pltpu.SemaphoreType.DMA((CHIPS,))] * 2
+        + [pairs] * 8
         + [pltpu.SemaphoreType.DMA((3, 2 * SIDE))] * 2,
         compiler_params=pltpu.CompilerParams(
             collective_id=0, has_side_effects=True, vmem_limit_bytes=56 * 1024 * 1024

time: 258 us -> 215 us (0.83)
  Pallas kernels: 245 us -> 201 us
    pallas_call x1, Pallas kernels: 132 us -> 107 us  [wide(): pl.pallas_call(functools.partial(wide_kernel, inv_root), out_shape=(jax.S...]
    pallas_call x1, Pallas kernels: 113 us -> 94 us  [layers(): pl.pallas_call(functools.partial(layers_kernel, 1e-05), out_shape=(jax.Sh...]
where the time goes in v3:
time: 215 us
  Pallas kernels  201 us (93%)
  local copies, waits for them, and re-layouts  8.77 us (4%)
  between operations  2.45 us (1%)
    pallas_call x1, Pallas kernels, wide(): pl.pallas_call(functools.partial(wide_kernel, inv_root), out_shape=(jax.S...  107 us
    pallas_call x1, Pallas kernels, layers(): pl.pallas_call(functools.partial(layers_kernel, 1e-05), out_shape=(jax.Sh...  94 us
    unnamed x9, local copies, waits for them, and re-layouts  8.04 us

profile of v3, /device:TPU:1, one launch (start us, length us, event | category | flops | bytes accessed | tf_op | source)
XLA Modules:
  0.0 214.6 jit_solution(4341588717224706508)
XLA Ops:
  0.6 0.8 reduce
  1.5 0.7 broadcast_in_dim.2.scale_ref
  2.2 0.0 copy-start
  2.2 2.2 %copy-done = bf16[128,16384]{1,0:T(8,128)(2,1)S(1)} copy-done((bf16[128,16384]{1,0:T(8,128)(2,1)S(1)}, bf16[128,16384]{1,0:T(8,128)(2,1)}, u32[]{:S(2)}) %copy-start) | copy-done | bytes 4194328
  4.4 0.0 copy-start.2
  4.4 1.0 copy-done.2
  5.5 94.0 %shard_map.95 = (bf16[128,2048]{1,0:T(8,128)(2,1)S(1)}, bf16[4096,128]{1,0:T(8,128)(2,1)S(1)}) custom-call(bf16[128,2048]{1,0:T(8,128)(2,1)S(1)} %copy-done.2, bf16[4,4,4,2,64,512]{5,4,3,2,1,0:T(8,128)(2,1)} %bitcast.4, bf16[4,4,2,16,8192]{4,3,2,1,0:T(8,128)(2,1)} %bitcast.5, bf16[4,16,128]{2,1,0:T(8,128)(2,1)S(1)} %bitcast.3, ...), custom_call_target="tpu_custom_call" | custom-call | tf_op jit(solution)/shard_map/pallas_call | solution.py:411
  99.5 0.0 copy-start.1
  99.5 1.0 copy-done.1
  100.4 0.0 copy-start.3
  100.5 0.8 copy-done.3
  101.2 107.2 %shard_map.96 = (bf16[2048,512]{1,0:T(8,128)(2,1)}, f32[8,128]{1,0:T(8,128)}) custom-call(bf16[128,2048]{1,0:T(8,128)(2,1)} %copy-done.3, bf16[2048,512]{1,0:T(8,128)(2,1)} %proj_ref.1, bf16[4096,128]{1,0:T(8,128)(2,1)} %copy-done.1, s32[4096]{0:T(1024)} %perm_ref.1), custom_call_target="tpu_custom_call" | custom-call | tf_op jit(solution)/shard_map/pallas_call | solution.py:776
  208.4 1.3 reduce_sum.9
  210.4 3.0 %copy.11 = bf16[2048,512]{1,0:T(8,128)(2,1)} copy(bf16[2048,512]{1,0:T(8,128)(2,1)} %get-tuple-element.12) | data formatting | bytes 4194304
Async XLA Ops:
  2.2 2.2 %copy-start = (bf16[128,16384]{1,0:T(8,128)(2,1)S(1)}, bf16[128,16384]{1,0:T(8,128)(2,1)}, u32[]{:S(2)}) copy-start(bf16[128,16384]{1,0:T(8,128)(2,1)} %codes_ref.1) | copy-start | bytes 12582916
  4.4 1.0 copy-start.2
  99.5 1.0 copy-start.1
  100.4 0.8 copy-start.3

commit v4 on v3

--- a/solution.py
+++ b/solution.py
@@ -33,7 +33,7 @@
     return (x * SIDE + y) * 2 + core
 
 
-def layers_kernel(
+def run_layers(
     eps,
     h_ref,
     value_ref,
@@ -45,7 +45,10 @@
     store_ref,
     w_value,
     w_out,
+    gain_row,
+    gain_own,
     gains,
+    scale_row,
     products,
     normed,
     values,
@@ -53,7 +56,6 @@
     in1,
     out2,
     in2,
-    stage,
     staged,
     own_sem,
     first_send,
@@ -79,26 +81,27 @@
     x, y, core = place(dp)
     sibling = dp + 1 - 2 * core
     zpair = (z + 1 - 2 * lax.rem(z, 2), 3 - z)
-    rows, features = h_ref.shape
+    rows, features = hidden_ref.shape
     head = value_ref.shape[-1]
     half = rows // 2
     weights = (w_value, w_out)
     width = 4 * features
 
-    barrier = pltpu.get_barrier_semaphore()
-
-    def greet(j, carry):
-        pl.semaphore_signal(
-            barrier, inc=1, device_id=(lax.rem(dp + j, RANKS), z), device_id_type=MESH
-        )
-        return carry
-
-    lax.fori_loop(1, RANKS, greet, 0)
-    for j in range(1, 4):
-        pl.semaphore_signal(
-            barrier, inc=1, device_id=(dp, lax.rem(z + j, 4)), device_id_type=MESH
-        )
-    pl.semaphore_wait(barrier, RANKS + 2)
+    def greet_all():
+        barrier = pltpu.get_barrier_semaphore()
+
+        def greet(j, carry):
+            pl.semaphore_signal(
+                barrier, inc=1, device_id=(lax.rem(dp + j, RANKS), z), device_id_type=MESH
+            )
+            return carry
+
+        lax.fori_loop(1, RANKS, greet, 0)
+        for j in range(1, 4):
+            pl.semaphore_signal(
+                barrier, inc=1, device_id=(dp, lax.rem(z + j, 4)), device_id_type=MESH
+            )
+        pl.semaphore_wait(barrier, RANKS + 2)
 
     def first_copy(kind, j):
         to = lax.rem(z + j, 4)
@@ -171,7 +174,7 @@
     def gain_copy(j):
         to = lax.rem(z + j, 4)
         return pltpu.make_async_remote_copy(
-            src_ref=gain_ref.at[to],
+            src_ref=gain_own.at[to],
             dst_ref=gains.at[4 - j],
             send_sem=gain_send.at[j - 1],
             recv_sem=gain_recv.at[3 - j],
@@ -188,7 +191,7 @@
 
     def stage_copy(d):
         columns = pl.ds(pl.multiple_of((d * 4 + z) * LANES, LANES), LANES)
-        return pltpu.make_async_copy(codes_ref.at[:, columns], stage.at[d], stage_sem.at[d])
+        return pltpu.make_async_copy(codes_ref.at[:, columns], staged.at[d], stage_sem.at[d])
 
     def code_copy(d):
         return pltpu.make_async_remote_copy(
@@ -225,10 +228,17 @@
             device_id_type=MESH,
         )
 
-    for j in range(1, 4):
+    small = (
+        pltpu.make_async_copy(gain_ref, gain_row, own_sem.at[2]),
+        pltpu.make_async_copy(scale_ref, scale_row, own_sem.at[3]),
+        pltpu.make_async_copy(h_ref, hidden_ref, own_sem.at[4]),
+    )
+    for copy in small:
+        copy.start()
+    greet_all()
+    for j in (1, 3, 2):
         first_copy(0, j).start()
         first_copy(1, j).start()
-        gain_copy(j).start()
     for copy in own_copies():
         copy.start()
 
@@ -237,12 +247,20 @@
         return carry
 
     lax.fori_loop(0, RANKS, fetch, 0)
-    gains[0] = gain_ref[z]
-    hidden_ref[...] = h_ref[...]
+    for copy in small:
+        copy.wait()
+    for part in range(4):
+        for j in range(features // LANES):
+            at = part * features + j * LANES
+            gain_own[part, j : j + 1, :] = gain_row[:, at : at + LANES]
+    for j in range(1, 4):
+        gain_copy(j).start()
+    gains[0] = gain_own[z]
+    scale = jnp.broadcast_to(scale_row[...].astype(jnp.float32), (rows, LANES)).T
 
     def scale_codes(d, carry):
         stage_copy(d).wait()
-        staged[d] = (stage[d].astype(jnp.float32) * scale_ref[...]).astype(jnp.bfloat16)
+        staged[d] = (staged[d].astype(jnp.float32) * scale).astype(jnp.bfloat16)
         return carry
 
     lax.fori_loop(0, RANKS, scale_codes, 0)
@@ -375,12 +393,6 @@
 
     lax.fori_loop(0, 4, layer_step, 0)
 
-    def finish(j, carry):
-        code_arrival(lax.rem(dp + j, RANKS)).wait_recv()
-        code_copy(lax.rem(dp + j, RANKS)).wait_send()
-        return carry
-
-    lax.fori_loop(1, RANKS, finish, 0)
     for k in range(2):
         for layer in range(4):
             sum_copy(0, layer, k).wait_send()
@@ -396,73 +408,34 @@
             for j in range(SIDE):
                 side_copy(kind, r, j, core).wait_send()
 
-
-def layers(hidden, value_weight, folded_out, gain, codes, scales):
-    rows, features = hidden.shape
-    head = value_weight.shape[1]
-    half = rows // 2
-    grid = (4, SIDE, SIDE, 2)
-    value_weight = value_weight.reshape(*grid, features // RANKS, head)
-    folded_out = folded_out.reshape(*grid[1:], head // RANKS, 4 * features)
-    vmem = pl.BlockSpec(memory_space=pltpu.VMEM)
-    anywhere = pl.BlockSpec(memory_space=pl.ANY)
-    dma = pltpu.SemaphoreType.DMA
-    message = (4, 2, half, head + LANES)
-    return pl.pallas_call(
-        functools.partial(layers_kernel, 1e-5),
-        out_shape=(
-            jax.ShapeDtypeStruct((rows, features), jnp.bfloat16),
-            jax.ShapeDtypeStruct((rows * RANKS, LANES), jnp.bfloat16),
-        ),
-        in_specs=[vmem, anywhere, anywhere, vmem, anywhere, vmem],
-        out_specs=(vmem, vmem),
-        scratch_shapes=[
-            pltpu.VMEM((*grid, features // RANKS, head), jnp.bfloat16),
-            pltpu.VMEM((*grid, head // RANKS, features), jnp.bfloat16),
-            pltpu.VMEM((4, features // LANES, LANES), jnp.bfloat16),
-            pltpu.VMEM((rows, head + LANES), jnp.float32),
-            pltpu.VMEM((rows, features), jnp.bfloat16),
-            pltpu.VMEM((rows, head), jnp.bfloat16),
-            pltpu.VMEM(message, jnp.bfloat16),
-            pltpu.VMEM(message, jnp.bfloat16),
-            pltpu.VMEM(message, jnp.bfloat16),
-            pltpu.VMEM(message, jnp.bfloat16),
-            pltpu.VMEM((RANKS, rows, LANES), jnp.bfloat16),
-            pltpu.VMEM((RANKS, rows, LANES), jnp.bfloat16),
-            dma((2,)),
-            dma((2, 3)),
-            dma((2, 3)),
-            dma((2, 3, SIDE)),
-            dma((2, 3, SIDE)),
-            dma((2, 3, SIDE)),
-            dma((2, 3, SIDE)),
-            dma((2, 3, SIDE)),
-            dma((2, 3, SIDE)),
-            dma((3,)),
-            dma((3,)),
-            dma((4, 2)),
-            dma((4, 2)),
-            dma((4, 2)),
-            dma((4, 2)),
-            dma((RANKS,)),
-            dma((RANKS,)),
-            dma((RANKS,)),
-        ],
-        compiler_params=pltpu.CompilerParams(
-            collective_id=1, has_side_effects=True, vmem_limit_bytes=40 * 1024 * 1024
-        ),
-    )(hidden, value_weight, folded_out, gain, codes, scales)
-
-
-def wide_kernel(
+    def codes_in():
+        def arrive(j, carry):
+            code_arrival(lax.rem(dp + j, RANKS)).wait_recv()
+            return carry
+
+        lax.fori_loop(1, RANKS, arrive, 0)
+
+    def codes_out():
+        def leave(j, carry):
+            code_copy(lax.rem(dp + j, RANKS)).wait_send()
+            return carry
+
+        lax.fori_loop(1, RANKS, leave, 0)
+
+    return codes_in, codes_out
+
+
+def run_wide(
     inv_root,
-    h_ref,
-    proj_ref,
+    share,
+    codes_in,
     store_ref,
     perm_ref,
+    proj_ref,
     grad_ref,
     loss_ref,
     held,
+    squares,
     total,
     y_own,
     y_keep,
@@ -474,7 +447,6 @@
     store,
     aim,
     losses,
-    own_sem,
     ring_send,
     ring_recv,
     side_send,
@@ -500,7 +472,7 @@
     za = z + 1 - 2 * lax.rem(z, 2)
     zb = 3 - z
     steps = CHIPS
-    part = h_ref.shape[0] // 2
+    part = held.shape[1] // 4
     block = 4 * part
     half = block // 2
     zpair = (za, zb)
@@ -517,19 +489,8 @@
             return (x * SIDE + spot) * 2 + core, z
         return ((spot // 2) * SIDE + y) * 2 + lax.rem(spot, 2), z
 
-    barrier = pltpu.get_barrier_semaphore()
-    for device in ((after, z), (before, z)):
-        pl.semaphore_signal(barrier, inc=1, device_id=device, device_id_type=MESH)
-    for group in range(3):
-        for j in range(1, sizes[group]):
-            pl.semaphore_signal(barrier, inc=1, device_id=peer(group, j), device_id_type=MESH)
-    pl.semaphore_wait(barrier, 2 + sum(sizes) - 3)
-
     mine = pl.multiple_of(core * 2 * part, 2 * part)
     theirs = pl.multiple_of((1 - core) * 2 * part, 2 * part)
-
-    def own_copy():
-        return pltpu.make_async_copy(h_ref, held.at[0, pl.ds(mine, 2 * part)], own_sem)
 
     def ring_copy(s, way, sub, later):
         start = mine + way * part + sub * (part // 2)
@@ -607,22 +568,19 @@
         )
 
     def loss_out(group):
-        losses[group, spots[group]] = loss_ref[...]
+        losses[group, spots[group]] = squares[...]
         for j in range(1, sizes[group]):
             loss_copy(group, j, False).start()
 
     def loss_in(group):
         for j in range(1, sizes[group]):
             loss_copy(group, j, True).wait_recv()
-        loss_ref[...] = functools.reduce(
+        squares[...] = functools.reduce(
             jnp.add, [losses[group, spot] for spot in range(sizes[group])]
         )
 
-    store[...] = store_ref[...].astype(jnp.float32)
-    loss_ref[...] = jnp.zeros_like(loss_ref)
+    squares[...] = jnp.zeros_like(squares)
     total[...] = jnp.zeros_like(total)
-    own_copy().start()
-    own_copy().wait()
 
     def pass_on(i, sub):
         @pl.when(jnp.logical_and(i > 0, i < steps))
@@ -656,27 +614,14 @@
                 out1[s, k, 1] = y_own[slot, other, rows, :].astype(jnp.bfloat16)
                 sum1_copy(s, k).start()
 
-        @pl.when(jnp.logical_and(i >= 2, i < steps + 2))
-        def _():
-            s = i - 2
-            slot = lax.rem(s, 2)
-            for k in range(2):
-                rows = pl.ds(k * half, half)
-                sum1_copy(s, k).wait_recv()
-                passed = y_own[slot, zpair[1 - k], rows, :] + in1[s, k, 1].astype(jnp.float32)
-                out2[s, k] = passed.astype(jnp.bfloat16)
-                sum2_copy(s, k).start()
-                y_keep[slot, rows, :] = y_own[slot, z, rows, :] + in1[s, k, 0].astype(jnp.float32)
-
-        pass_on(i, 1)
-
-        @pl.when(i < steps)
-        def _():
-            side_copy(i, mine).start()
-
-        @pl.when(jnp.logical_and(i >= 3, i < steps + 3))
-        def _():
-            s = i - 3
+        @pl.when(i == 4)
+        def _():
+            codes_in()
+            store[...] = store_ref[...].astype(jnp.float32)
+
+        @pl.when(jnp.logical_and(i >= 4, i < steps + 4))
+        def _():
+            s = i - 4
             slot = lax.rem(s, 2)
             for k in range(2):
                 sum2_copy(s, k).wait_recv()
@@ -703,13 +648,31 @@
                     - aim[rows, :]
                 )
                 rows_g[s, z, rows, :] = (diff * inv_root).astype(jnp.bfloat16)
-                loss_ref[...] += jnp.sum((diff * diff).reshape(part // 8, 8, diff.shape[1]), axis=0)
+                squares[...] += jnp.sum((diff * diff).reshape(part // 8, 8, diff.shape[1]), axis=0)
             for k in range(2):
                 rows1_copy(s, k, z).start()
 
-        @pl.when(jnp.logical_and(i >= 4, i < steps + 4))
-        def _():
-            s = i - 4
+        pass_on(i, 1)
+
+        @pl.when(i < steps)
+        def _():
+            side_copy(i, mine).start()
+
+        @pl.when(jnp.logical_and(i >= 2, i < steps + 2))
+        def _():
+            s = i - 2
+            slot = lax.rem(s, 2)
+            for k in range(2):
+                rows = pl.ds(k * half, half)
+                sum1_copy(s, k).wait_recv()
+                passed = y_own[slot, zpair[1 - k], rows, :] + in1[s, k, 1].astype(jnp.float32)
+                out2[s, k] = passed.astype(jnp.bfloat16)
+                sum2_copy(s, k).start()
+                y_keep[slot, rows, :] = y_own[slot, z, rows, :] + in1[s, k, 0].astype(jnp.float32)
+
+        @pl.when(jnp.logical_and(i >= 5, i < steps + 5))
+        def _():
+            s = i - 5
             for k in range(2):
                 rows1_copy(s, k, zpair[k]).wait_recv()
             for k in range(2):
@@ -724,9 +687,14 @@
             loss_in(0)
             loss_out(1)
 
-        @pl.when(i >= 5)
-        def _():
-            s = i - 5
+        @pl.when(i == steps + 5)
+        def _():
+            loss_in(1)
+            loss_out(2)
+
+        @pl.when(i >= 6)
+        def _():
+            s = i - 6
             for k in range(2):
                 rows2_copy(s, k, 3 - zpair[k] if k == 0 else zpair[k] + 1 - 2 * lax.rem(zpair[k], 2)).wait_recv()
             rows = jnp.concatenate([rows_g[s, q] for q in range(4)], axis=1)
@@ -738,9 +706,7 @@
 
         return carry
 
-    lax.fori_loop(0, steps + 5, body, 0)
-    loss_in(1)
-    loss_out(2)
+    lax.fori_loop(0, steps + 6, body, 0)
 
     def finish(s, carry):
         @pl.when(s < steps - 1)
@@ -763,65 +729,171 @@
         for j in range(1, sizes[group]):
             loss_copy(group, j, False).wait_send()
     grad_ref[...] = total[...].astype(jnp.bfloat16)
-
-
-def wide(hidden, proj, store, perm, inv_root):
+    loss_ref[0, 0] = jnp.sum(squares[...]) * share
+
+
+LAYER_SCRATCH = 32
+
+
+def kernel(
+    eps,
+    inv_root,
+    share,
+    h_ref,
+    value_ref,
+    out_ref,
+    gain_ref,
+    proj_ref,
+    codes_ref,
+    scale_ref,
+    perm_ref,
+    grad_ref,
+    loss_ref,
+    held,
+    store_ref,
+    proj,
+    proj_sem,
+    *scratch,
+):
+    core = lax.rem(lax.axis_index("dp"), 2)
+    rows = held.shape[1] // 2
+    fetch_proj = pltpu.make_async_copy(proj_ref, proj, proj_sem)
+    fetch_proj.start()
+    codes_in, codes_out = run_layers(
+        eps,
+        h_ref,
+        value_ref,
+        out_ref,
+        gain_ref,
+        codes_ref,
+        scale_ref,
+        held.at[0, pl.ds(pl.multiple_of(core * rows, rows), rows)],
+        store_ref,
+        *scratch[:LAYER_SCRATCH],
+    )
+    fetch_proj.wait()
+    run_wide(
+        inv_root,
+        share,
+        codes_in,
+        store_ref,
+        perm_ref,
+        proj,
+        grad_ref,
+        loss_ref,
+        held,
+        *scratch[LAYER_SCRATCH:],
+    )
+    codes_out()
+
+
+def distill(hidden, value_weight, folded_out, gain, proj, codes, scales, perm):
     rows, features = hidden.shape
+    head = value_weight.shape[1]
     columns = proj.shape[1]
     quarter = columns // 4
+    tokens = rows * RANKS
     block = 2 * rows
-    half = block // 2
-    pairs = pltpu.SemaphoreType.DMA((CHIPS, 2))
+    wide_half = block // 2
+    half = rows // 2
+    grid = (4, SIDE, SIDE, 2)
+    value_weight = value_weight.reshape(*grid, features // RANKS, head)
+    folded_out = folded_out.reshape(*grid[1:], head // RANKS, 4 * features)
+    bf16, f32 = jnp.bfloat16, jnp.float32
+    dma = pltpu.SemaphoreType.DMA
+    message = pltpu.VMEM((4, 2, half, head + LANES), bf16)
+    lanes = (features // LANES, LANES)
+    layer_scratch = [
+        pltpu.VMEM((*grid, features // RANKS, head), bf16),
+        pltpu.VMEM((*grid, head // RANKS, features), bf16),
+        pltpu.VMEM(gain.shape, bf16),
+        pltpu.VMEM((4, *lanes), bf16),
+        pltpu.VMEM((4, *lanes), bf16),
+        pltpu.VMEM(scales.shape, bf16),
+        pltpu.VMEM((rows, head + LANES), f32),
+        pltpu.VMEM((rows, features), bf16),
+        pltpu.VMEM((rows, head), bf16),
+        message,
+        message,
+        message,
+        message,
+        pltpu.VMEM((RANKS, rows, LANES), bf16),
+        dma((5,)),
+        dma((2, 3)),
+        dma((2, 3)),
+        *[dma((2, 3, SIDE))] * 6,
+        dma((3,)),
+        dma((3,)),
+        *[dma((4, 2))] * 4,
+        *[dma((RANKS,))] * 3,
+    ]
+    wide_scratch = [
+        pltpu.VMEM((8, quarter), f32),
+        pltpu.VMEM((features, columns), f32),
+        pltpu.VMEM((2, 4, block, quarter), f32),
+        pltpu.VMEM((2, block, quarter), f32),
+        pltpu.VMEM((CHIPS, 2, 2, wide_half, quarter), bf16),
+        pltpu.VMEM((CHIPS, 2, 2, wide_half, quarter), bf16),
+        pltpu.VMEM((CHIPS, 2, wide_half, quarter), bf16),
+        pltpu.VMEM((CHIPS, 2, wide_half, quarter), bf16),
+        pltpu.VMEM((CHIPS, 4, block, quarter), bf16),
+        pltpu.VMEM((tokens, LANES), f32),
+        pltpu.VMEM((block, quarter), f32),
+        pltpu.VMEM((3, 2 * SIDE, 8, quarter), f32),
+        dma((CHIPS, 2, 2)),
+        dma((CHIPS, 2, 2)),
+        dma((CHIPS,)),
+        dma((CHIPS,)),
+        dma((CHIPS, 2)),
+        dma((CHIPS, 2)),
+        dma((CHIPS, 2)),
+        dma((CHIPS, 2)),
+        dma((CHIPS, 2)),
+        dma((CHIPS, 2)),
+        dma((CHIPS, 2)),
+        dma((CHIPS, 2)),
+        dma((3, 2 * SIDE)),
+        dma((3, 2 * SIDE)),
+    ]
     vmem = pl.BlockSpec(memory_space=pltpu.VMEM)
+    smem = pl.BlockSpec(memory_space=pltpu.SMEM)
+    anywhere = pl.BlockSpec(memory_space=pl.ANY)
     return pl.pallas_call(
-        functools.partial(wide_kernel, inv_root),
+        functools.partial(kernel, 1e-5, 1.0 / math.sqrt(tokens), 0.5 / (tokens * columns * RANKS)),
         out_shape=(
-            jax.ShapeDtypeStruct((features, columns), jnp.bfloat16),
-            jax.ShapeDtypeStruct((8, quarter), jnp.float32),
+            jax.ShapeDtypeStruct((features, columns), bf16),
+            jax.ShapeDtypeStruct((1, 1), f32),
         ),
-        in_specs=[vmem, vmem, vmem, pl.BlockSpec(memory_space=pltpu.SMEM)],
-        out_specs=(vmem, vmem),
+        in_specs=[anywhere] * 7 + [smem],
+        out_specs=(vmem, smem),
         scratch_shapes=[
-            pltpu.VMEM((CHIPS, block, features), jnp.bfloat16),
-            pltpu.VMEM((features, columns), jnp.float32),
-            pltpu.VMEM((2, 4, block, quarter), jnp.float32),
-            pltpu.VMEM((2, block, quarter), jnp.float32),
-            pltpu.VMEM((CHIPS, 2, 2, half, quarter), jnp.bfloat16),
-            pltpu.VMEM((CHIPS, 2, 2, half, quarter), jnp.bfloat16),
-            pltpu.VMEM((CHIPS, 2, half, quarter), jnp.bfloat16),
-            pltpu.VMEM((CHIPS, 2, half, quarter), jnp.bfloat16),
-            pltpu.VMEM((CHIPS, 4, block, quarter), jnp.bfloat16),
-            pltpu.VMEM(store.shape, jnp.float32),
-            pltpu.VMEM((block, quarter), jnp.float32),
-            pltpu.VMEM((3, 2 * SIDE, 8, quarter), jnp.float32),
-            pltpu.SemaphoreType.DMA,
+            pltpu.VMEM((CHIPS, block, features), bf16),
+            pltpu.VMEM((tokens, LANES), bf16),
+            pltpu.VMEM(proj.shape, bf16),
+            dma,
         ]
-        + [pltpu.SemaphoreType.DMA((CHIPS, 2, 2))] * 2
-        + [pltpu.SemaphoreType.DMA((CHIPS,))] * 2
-        + [pairs] * 8
-        + [pltpu.SemaphoreType.DMA((3, 2 * SIDE))] * 2,
+        + layer_scratch
+        + wide_scratch,
         compiler_params=pltpu.CompilerParams(
-            collective_id=0, has_side_effects=True, vmem_limit_bytes=56 * 1024 * 1024
+            collective_id=0, has_side_effects=True, vmem_limit_bytes=63 * 1024 * 1024
         ),
-    )(hidden, proj, store, perm)
+    )(hidden, value_weight, folded_out, gain, proj, codes, scales, perm)
 
 
 def shards(
     student_in, value_weight, folded_out, norm_gain, proj, teacher_codes, teacher_scales, perm
 ):
-    sections = lax.axis_size("pipe")
-    n_ranks = lax.axis_size("dp")
-    rows, features = student_in.shape
-    tokens = rows * n_ranks
-    columns = proj.shape[1]
-    total_cols = columns * n_ranks
-
-    gain = norm_gain.reshape(sections, features // LANES, LANES)
-    scales = jnp.broadcast_to(teacher_scales.astype(jnp.float32)[:, None], (rows, LANES))
-    hidden, store = layers(student_in, value_weight[0], folded_out[0], gain, teacher_codes, scales)
-    grad_proj, squared = wide(hidden, proj, store, perm, 1.0 / math.sqrt(tokens))
-    loss = 0.5 * jnp.sum(squared) / (tokens * total_cols)
-    return (grad_proj, loss)
+    grad_proj, loss = distill(
+        student_in,
+        value_weight[0],
+        folded_out[0],
+        norm_gain,
+        proj,
+        teacher_codes,
+        teacher_scales[None, :],
+        perm,
+    )
+    return (grad_proj, loss[0, 0])
 
 
 def solution(mesh):

time: 215 us -> 199 us (0.926)
  Pallas kernels: 201 us -> 194 us
  local copies, waits for them, and re-layouts: 8.77 us -> 3.05 us
    pallas_call x2 -> x1, Pallas kernels: 201 us -> 194 us  [distill(): pl.pallas_call(functools.partial(kernel, 1e-05, 1.0 / math.sqrt(tokens),...]
    unnamed x9 -> x1, local copies, waits for them, and re-layouts: 8.04 us -> 3.05 us
where the time goes in v4:
time: 199 us
  Pallas kernels  194 us (97%)
  local copies, waits for them, and re-layouts  3.05 us (2%)
  between operations  2.38 us (1%)
    pallas_call x1, Pallas kernels, distill(): pl.pallas_call(functools.partial(kernel, 1e-05, 1.0 / math.sqrt(tokens),...  194 us

profile of v4, /device:TPU:1, one launch (start us, length us, event | category | flops | bytes accessed | tf_op | source)
XLA Modules:
  0.0 199.1 jit_solution(7124312553422945969)
XLA Ops:
  0.6 193.7 %shard_map.95 = (bf16[2048,512]{1,0:T(8,128)(2,1)}, f32[1,1]{1,0:T(1,128)}) custom-call(bf16[128,2048]{1,0:T(8,128)(2,1)} %h_ref.1, bf16[4,4,4,2,64,512]{5,4,3,2,1,0:T(8,128)(2,1)} %bitcast.4, bf16[4,4,2,16,8192]{4,3,2,1,0:T(8,128)(2,1)} %bitcast.5, bf16[1,8192]{1,0:T(2,128)(2,1)} %gain_ref.1, bf16[2048,512]{1,0:T(8,128)(2,1)} %proj_ref.1, ...), custom_call_target="tpu_custom_call" | custom-call | tf_op jit(solution)/shard_map/pallas_call | solution.py:861
  194.3 3.0 %copy.12 = bf16[2048,512]{1,0:T(8,128)(2,1)} copy(bf16[2048,512]{1,0:T(8,128)(2,1)} %get-tuple-element.8) | data formatting | bytes 4194304

commit v5 on v4

--- a/solution.py
+++ b/solution.py
@@ -60,6 +60,7 @@
     own_sem,
     first_send,
     first_recv,
+    late_send,
     near_send,
     near_recv,
     far_send,
@@ -159,6 +160,27 @@
             device_id_type=MESH,
         )
 
+    def late_copy(kind, j):
+        to = lax.rem(z + j, 4)
+        at = lax.rem(spot[1 - kind] + 2, SIDE)
+        if kind == 0:
+            source = value_ref.at[to, :, at, core]
+            target = w_value.at[4 - j, :, at, core]
+        else:
+            source = out_ref.at[at, :, core, :, pl.ds(pl.multiple_of(to * features, features), features)]
+            target = w_out.at[4 - j, at, :, core]
+        return pltpu.make_async_remote_copy(
+            src_ref=source,
+            dst_ref=target,
+            send_sem=late_send.at[kind, j - 1],
+            recv_sem=far_recv.at[kind, 3 - j, at],
+            device_id=(dp, to),
+            device_id_type=MESH,
+        )
+
+    def is_late(j):
+        return z + jnp.where(z < lax.rem(z + j, 4), 1, 0) > 1
+
     def side_copy(kind, r, j, owner):
         at = lax.rem(spot[1 - kind] + j, SIDE)
         block = w_value.at[r, :, at, owner] if kind == 0 else w_out.at[r, at, :, owner]
@@ -239,6 +261,13 @@
     for j in (1, 3, 2):
         first_copy(0, j).start()
         first_copy(1, j).start()
+    for j in (1, 3, 2):
+
+        @pl.when(is_late(j))
+        def _():
+            for kind in range(2):
+                late_copy(kind, j).start()
+
     for copy in own_copies():
         copy.start()
 
@@ -283,8 +312,13 @@
         for kind in range(2):
             for j in (1, 3, 2):
                 near_copy(kind, r, j, True).wait_recv()
-            for j in (1, 3, 2):
+            for j in (1, 3):
                 far_copy(kind, r, j, False).start()
+
+            @pl.when(k == 0)
+            def _():
+                far_copy(kind, r, 2, False).start()
+
         for kind in range(2):
             side_copy(kind, r, 0, core).start()
 
@@ -397,12 +431,19 @@
         for layer in range(4):
             sum_copy(0, layer, k).wait_send()
             sum_copy(1, layer, k).wait_send()
-    for j in range(1, 4):
-        for kind in range(2):
+    for kind in range(2):
+        for j in range(1, 4):
             first_copy(kind, j).wait_send()
             for r in range(1, 4):
                 near_copy(kind, r, j, False).wait_send()
-                far_copy(kind, r, j, False).wait_send()
+                if j != 2:
+                    far_copy(kind, r, j, False).wait_send()
+
+            @pl.when(is_late(j))
+            def _():
+                late_copy(kind, j).wait_send()
+
+        far_copy(kind, turn(0), 2, False).wait_send()
     for kind in range(2):
         for r in range(1, 4):
             for j in range(SIDE):
@@ -493,8 +534,8 @@
     theirs = pl.multiple_of((1 - core) * 2 * part, 2 * part)
 
     def ring_copy(s, way, sub, later):
-        start = mine + way * part + sub * (part // 2)
-        rows = pl.ds(pl.multiple_of(start, part // 2), part // 2)
+        start = mine + way * part + sub * (part // 4)
+        rows = pl.ds(pl.multiple_of(start, part // 4), part // 4)
         return pltpu.make_async_remote_copy(
             src_ref=held.at[s, rows],
             dst_ref=held.at[s + later, rows],
@@ -614,6 +655,8 @@
                 out1[s, k, 1] = y_own[slot, other, rows, :].astype(jnp.bfloat16)
                 sum1_copy(s, k).start()
 
+        pass_on(i, 1)
+
         @pl.when(i == 4)
         def _():
             codes_in()
@@ -652,11 +695,7 @@
             for k in range(2):
                 rows1_copy(s, k, z).start()
 
-        pass_on(i, 1)
-
-        @pl.when(i < steps)
-        def _():
-            side_copy(i, mine).start()
+        pass_on(i, 2)
 
         @pl.when(jnp.logical_and(i >= 2, i < steps + 2))
         def _():
@@ -678,6 +717,12 @@
             for k in range(2):
                 rows2_copy(s, k, zpair[1 - k]).start()
 
+        pass_on(i, 3)
+
+        @pl.when(i < steps)
+        def _():
+            side_copy(i, mine).start()
+
         @pl.when(i == steps + 3)
         def _():
             loss_out(0)
@@ -712,7 +757,7 @@
         @pl.when(s < steps - 1)
         def _():
             for way in range(2):
-                for sub in range(2):
+                for sub in range(4):
                     ring_copy(s, way, sub, 1).wait_send()
 
         side_copy(s, mine).wait_send()
@@ -732,7 +777,7 @@
     loss_ref[0, 0] = jnp.sum(squares[...]) * share
 
 
-LAYER_SCRATCH = 32
+LAYER_SCRATCH = 33
 
 
 def kernel(
@@ -819,8 +864,7 @@
         message,
         pltpu.VMEM((RANKS, rows, LANES), bf16),
         dma((5,)),
-        dma((2, 3)),
-        dma((2, 3)),
+        *[dma((2, 3))] * 3,
         *[dma((2, 3, SIDE))] * 6,
         dma((3,)),
         dma((3,)),
@@ -840,8 +884,8 @@
         pltpu.VMEM((tokens, LANES), f32),
         pltpu.VMEM((block, quarter), f32),
         pltpu.VMEM((3, 2 * SIDE, 8, quarter), f32),
-        dma((CHIPS, 2, 2)),
-        dma((CHIPS, 2, 2)),
+        dma((CHIPS, 2, 4)),
+        dma((CHIPS, 2, 4)),
         dma((CHIPS,)),
         dma((CHIPS,)),
         dma((CHIPS, 2)),

time: 199 us -> 204 us (1.025)
  Pallas kernels: 194 us -> 199 us
    pallas_call x1, Pallas kernels: 194 us -> 199 us  [distill(): pl.pallas_call(functools.partial(kernel, 1e-05, 1.0 / math.sqrt(tokens),...]
where the time goes in v5:
time: 204 us
  Pallas kernels  199 us (98%)
  local copies, waits for them, and re-layouts  3.05 us (1%)
  between operations  2.38 us (1%)
    pallas_call x1, Pallas kernels, distill(): pl.pallas_call(functools.partial(kernel, 1e-05, 1.0 / math.sqrt(tokens),...  199 us

profile of v5, /device:TPU:1, one launch (start us, length us, event | category | flops | bytes accessed | tf_op | source)
XLA Modules:
  0.0 204.0 jit_solution(13278258351507785068)
XLA Ops:
  0.6 198.6 %shard_map.95 = (bf16[2048,512]{1,0:T(8,128)(2,1)}, f32[1,1]{1,0:T(1,128)}) custom-call(bf16[128,2048]{1,0:T(8,128)(2,1)} %h_ref.1, bf16[4,4,4,2,64,512]{5,4,3,2,1,0:T(8,128)(2,1)} %bitcast.4, bf16[4,4,2,16,8192]{4,3,2,1,0:T(8,128)(2,1)} %bitcast.5, bf16[1,8192]{1,0:T(2,128)(2,1)} %gain_ref.1, bf16[2048,512]{1,0:T(8,128)(2,1)} %proj_ref.1, ...), custom_call_target="tpu_custom_call" | custom-call | tf_op jit(solution)/shard_map/pallas_call | solution.py:905
  199.3 3.0 %copy.12 = bf16[2048,512]{1,0:T(8,128)(2,1)} copy(bf16[2048,512]{1,0:T(8,128)(2,1)} %get-tuple-element.8) | data formatting | bytes 4194304

commit v6 on v4

--- a/solution.py
+++ b/solution.py
@@ -84,6 +84,7 @@
     rows, features = hidden_ref.shape
     head = value_ref.shape[-1]
     half = rows // 2
+    quarter = rows // 4
     weights = (w_value, w_out)
     width = 4 * features
 
@@ -214,16 +215,16 @@
             device_id_type=MESH,
         )
 
-    def sum_copy(phase, layer, k):
+    def sum_copy(phase, layer, k, part):
         source, target, send, recv = (
             (out1, in1, sum1_send, sum1_recv),
             (out2, in2, sum2_send, sum2_recv),
         )[phase]
         return pltpu.make_async_remote_copy(
-            src_ref=source.at[layer, k],
-            dst_ref=target.at[layer, k],
-            send_sem=send.at[layer, k],
-            recv_sem=recv.at[layer, k],
+            src_ref=source.at[layer, k, part],
+            dst_ref=target.at[layer, k, part],
+            send_sem=send.at[layer, k, part],
+            recv_sem=recv.at[layer, k, part],
             device_id=(dp, zpair[k ^ phase]),
             device_id_type=MESH,
         )
@@ -256,16 +257,6 @@
     for j in range(1, 4):
         gain_copy(j).start()
     gains[0] = gain_own[z]
-    scale = jnp.broadcast_to(scale_row[...].astype(jnp.float32), (rows, LANES)).T
-
-    def scale_codes(d, carry):
-        stage_copy(d).wait()
-        staged[d] = (staged[d].astype(jnp.float32) * scale).astype(jnp.bfloat16)
-        return carry
-
-    lax.fori_loop(0, RANKS, scale_codes, 0)
-    store_ref[pl.ds(pl.multiple_of(dp * rows, rows), rows), :] = staged[dp]
-
     def turn(k):
         layer = k + jnp.where(k >= z, 1, 0)
         return lax.rem(layer - z + 4, 4)
@@ -296,6 +287,16 @@
 
     lax.fori_loop(0, 3, spread_near, 0)
     spread_far(0)
+    scale = jnp.broadcast_to(scale_row[...].astype(jnp.float32), (rows, LANES)).T
+
+    def scale_codes(d, carry):
+        stage_copy(d).wait()
+        staged[d] = (staged[d].astype(jnp.float32) * scale).astype(jnp.bfloat16)
+        return carry
+
+    lax.fori_loop(0, RANKS, scale_codes, 0)
+    store_ref[pl.ds(pl.multiple_of(dp * rows, rows), rows), :] = staged[dp]
+
     for copy in own_copies():
         copy.wait()
     for j in range(1, 4):
@@ -323,9 +324,9 @@
                 for j in range(SIDE):
                     side_copy(kind, r, j, 1 - core).wait_recv()
 
-            @pl.when(layer == 3 - jnp.where(z == 3, 1, 0))
-            def _():
-                lax.fori_loop(1, RANKS, send_codes, 0)
+        @pl.when(layer == 2)
+        def _():
+            lax.fori_loop(1, RANKS, send_codes, 0)
 
         gain = gains[r].astype(jnp.float32)
         squares = jnp.zeros((rows, LANES), jnp.float32)
@@ -335,50 +336,45 @@
             squares += tile * tile
             normed[:, columns] = (tile * gain[j : j + 1, :]).astype(jnp.bfloat16)
         squares = jnp.broadcast_to(jnp.sum(squares, axis=1, keepdims=True), (rows, LANES))
-        high = squares.astype(jnp.bfloat16)
-        low = (squares - high.astype(jnp.float32)).astype(jnp.bfloat16)
-        lane = lax.broadcasted_iota(jnp.int32, (rows, LANES), 1)
         products[:, :head] = jnp.dot(
             normed[...], w_value[r].reshape(features, head), preferred_element_type=jnp.float32
         )
         products[:, head:] = squares
-        for k in range(2):
-            part = slice(k * half, (k + 1) * half)
-            out1[layer, k, :, :head] = products[part, :head].astype(jnp.bfloat16)
-            out1[layer, k, :, head:] = jnp.where(
-                lane[part] < LANES // 2, high[part].astype(jnp.float32), low[part].astype(jnp.float32)
-            ).astype(jnp.bfloat16)
-            sum_copy(0, layer, k).start()
-
-        def arrived(buffer, k):
-            marks = buffer[layer, k, :, head:].astype(jnp.float32)
-            return buffer[layer, k, :, :head].astype(jnp.float32), marks + pltpu.roll(marks, LANES // 2, 1)
-
-        for k in range(2):
-            part = slice(k * half, (k + 1) * half)
-            sum_copy(0, layer, k).wait_recv()
-            more, marks = arrived(in1, k)
-            so_far = products[part, :head] + more
-            squares = products[part, head:] + marks
-            products[part, :head] = so_far
-            products[part, head:] = squares
-            high = squares.astype(jnp.bfloat16)
-            low = (squares - high.astype(jnp.float32)).astype(jnp.bfloat16)
-            out2[layer, k, :, :head] = so_far.astype(jnp.bfloat16)
-            out2[layer, k, :, head:] = jnp.where(
-                lane[part] < LANES // 2, high.astype(jnp.float32), low.astype(jnp.float32)
-            ).astype(jnp.bfloat16)
-            sum_copy(1, layer, k).start()
-        for k in range(2):
-            part = slice(k * half, (k + 1) * half)
-            sum_copy(1, layer, k).wait_recv()
-            more, marks = arrived(in2, k)
-            scale = lax.rsqrt((products[part, head:] + marks) * (1.0 / width) + eps)
+        lane = lax.broadcasted_iota(jnp.int32, (quarter, LANES), 1)
+
+        def leave(phase, k, part):
+            rows_in = slice(k * half + part * quarter, k * half + (part + 1) * quarter)
+            buffer = (out1, out2)[phase]
+            squares = products[rows_in, head:]
+            high = squares.astype(jnp.bfloat16).astype(jnp.float32)
+            buffer[layer, k, part, :, :head] = products[rows_in, :head].astype(jnp.bfloat16)
+            buffer[layer, k, part, :, head:] = jnp.where(lane < LANES // 2, high, squares - high).astype(
+                jnp.bfloat16
+            )
+            sum_copy(phase, layer, k, part).start()
+
+        def arrive(phase, k, part):
+            rows_in = slice(k * half + part * quarter, k * half + (part + 1) * quarter)
+            buffer = (in1, in2)[phase]
+            sum_copy(phase, layer, k, part).wait_recv()
+            marks = buffer[layer, k, part, :, head:].astype(jnp.float32)
+            so_far = products[rows_in, :head] + buffer[layer, k, part, :, :head].astype(jnp.float32)
+            return rows_in, so_far, products[rows_in, head:] + marks + pltpu.roll(marks, LANES // 2, 1)
+
+        order = [(k, part) for part in range(2) for k in range(2)]
+        for k, part in order:
+            leave(0, k, part)
+        for k, part in order:
+            rows_in, so_far, squares = arrive(0, k, part)
+            products[rows_in, :head] = so_far
+            products[rows_in, head:] = squares
+            leave(1, k, part)
+        for k, part in order:
+            rows_in, so_far, squares = arrive(1, k, part)
+            scale = lax.rsqrt(squares * (1.0 / width) + eps)
             for j in range(head // LANES):
                 columns = slice(j * LANES, (j + 1) * LANES)
-                values[part, columns] = ((products[part, columns] + more[:, columns]) * scale).astype(
-                    jnp.bfloat16
-                )
+                values[rows_in, columns] = (so_far[:, columns] * scale).astype(jnp.bfloat16)
         for n in range(features // 512):
             columns = slice(n * 512, (n + 1) * 512)
             branch = jnp.dot(
@@ -393,20 +389,21 @@
 
     lax.fori_loop(0, 4, layer_step, 0)
 
-    for k in range(2):
+    def sends_out():
+        for kind in range(2):
+            for j in range(1, 4):
+                first_copy(kind, j).wait_send()
+                for r in range(1, 4):
+                    near_copy(kind, r, j, False).wait_send()
+                    far_copy(kind, r, j, False).wait_send()
+            for r in range(1, 4):
+                for j in range(SIDE):
+                    side_copy(kind, r, j, core).wait_send()
         for layer in range(4):
-            sum_copy(0, layer, k).wait_send()
-            sum_copy(1, layer, k).wait_send()
-    for j in range(1, 4):
-        for kind in range(2):
-            first_copy(kind, j).wait_send()
-            for r in range(1, 4):
-                near_copy(kind, r, j, False).wait_send()
-                far_copy(kind, r, j, False).wait_send()
-    for kind in range(2):
-        for r in range(1, 4):
-            for j in range(SIDE):
-                side_copy(kind, r, j, core).wait_send()
+            for k in range(2):
+                for part in range(2):
+                    for phase in range(2):
+                        sum_copy(phase, layer, k, part).wait_send()
 
     def codes_in():
         def arrive(j, carry):
@@ -422,21 +419,22 @@
 
         lax.fori_loop(1, RANKS, leave, 0)
 
-    return codes_in, codes_out
+    return codes_in, codes_out, sends_out
 
 
 def run_wide(
     inv_root,
     share,
     codes_in,
+    codes_out,
+    sends_out,
     store_ref,
     perm_ref,
     proj_ref,
-    grad_ref,
+    total,
     loss_ref,
     held,
     squares,
-    total,
     y_own,
     y_keep,
     out1,
@@ -493,8 +491,8 @@
     theirs = pl.multiple_of((1 - core) * 2 * part, 2 * part)
 
     def ring_copy(s, way, sub, later):
-        start = mine + way * part + sub * (part // 2)
-        rows = pl.ds(pl.multiple_of(start, part // 2), part // 2)
+        start = mine + way * part + sub * (part // 4)
+        rows = pl.ds(pl.multiple_of(start, part // 4), part // 4)
         return pltpu.make_async_remote_copy(
             src_ref=held.at[s, rows],
             dst_ref=held.at[s + later, rows],
@@ -614,6 +612,8 @@
                 out1[s, k, 1] = y_own[slot, other, rows, :].astype(jnp.bfloat16)
                 sum1_copy(s, k).start()
 
+        pass_on(i, 1)
+
         @pl.when(i == 4)
         def _():
             codes_in()
@@ -652,11 +652,7 @@
             for k in range(2):
                 rows1_copy(s, k, z).start()
 
-        pass_on(i, 1)
-
-        @pl.when(i < steps)
-        def _():
-            side_copy(i, mine).start()
+        pass_on(i, 2)
 
         @pl.when(jnp.logical_and(i >= 2, i < steps + 2))
         def _():
@@ -678,6 +674,12 @@
             for k in range(2):
                 rows2_copy(s, k, zpair[1 - k]).start()
 
+        pass_on(i, 3)
+
+        @pl.when(i < steps)
+        def _():
+            side_copy(i, mine).start()
+
         @pl.when(i == steps + 3)
         def _():
             loss_out(0)
@@ -704,31 +706,35 @@
                     held[s, :, features], rows, (((0,), (0,)), ((), ())), preferred_element_type=jnp.float32
                 )
 
+            @pl.when(s < steps - 1)
+            def _():
+                for way in range(2):
+                    for sub in range(4):
+                        ring_copy(s, way, sub, 1).wait_send()
+
+            side_copy(s, mine).wait_send()
+            for k in range(2):
+                sum1_copy(s, k).wait_send()
+                sum2_copy(s, k).wait_send()
+                rows1_copy(s, k, z).wait_send()
+                rows2_copy(s, k, zpair[1 - k]).wait_send()
+
+        @pl.when(i == 8)
+        def _():
+            sends_out()
+
+        @pl.when(i == 10)
+        def _():
+            codes_out()
+
         return carry
 
     lax.fori_loop(0, steps + 6, body, 0)
 
-    def finish(s, carry):
-        @pl.when(s < steps - 1)
-        def _():
-            for way in range(2):
-                for sub in range(2):
-                    ring_copy(s, way, sub, 1).wait_send()
-
-        side_copy(s, mine).wait_send()
-        for k in range(2):
-            sum1_copy(s, k).wait_send()
-            sum2_copy(s, k).wait_send()
-            rows1_copy(s, k, z).wait_send()
-            rows2_copy(s, k, zpair[1 - k]).wait_send()
-        return carry
-
-    lax.fori_loop(0, steps, finish, 0)
     loss_in(2)
     for group in range(3):
         for j in range(1, sizes[group]):
             loss_copy(group, j, False).wait_send()
-    grad_ref[...] = total[...].astype(jnp.bfloat16)
     loss_ref[0, 0] = jnp.sum(squares[...]) * share
 
 
@@ -759,7 +765,7 @@
     rows = held.shape[1] // 2
     fetch_proj = pltpu.make_async_copy(proj_ref, proj, proj_sem)
     fetch_proj.start()
-    codes_in, codes_out = run_layers(
+    codes_in, codes_out, sends_out = run_layers(
         eps,
         h_ref,
         value_ref,
@@ -776,6 +782,8 @@
         inv_root,
         share,
         codes_in,
+        codes_out,
+        sends_out,
         store_ref,
         perm_ref,
         proj,
@@ -784,7 +792,6 @@
         held,
         *scratch[LAYER_SCRATCH:],
     )
-    codes_out()
 
 
 def distill(hidden, value_weight, folded_out, gain, proj, codes, scales, perm):
@@ -795,13 +802,12 @@
     tokens = rows * RANKS
     block = 2 * rows
     wide_half = block // 2
-    half = rows // 2
     grid = (4, SIDE, SIDE, 2)
     value_weight = value_weight.reshape(*grid, features // RANKS, head)
     folded_out = folded_out.reshape(*grid[1:], head // RANKS, 4 * features)
     bf16, f32 = jnp.bfloat16, jnp.float32
     dma = pltpu.SemaphoreType.DMA
-    message = pltpu.VMEM((4, 2, half, head + LANES), bf16)
+    message = pltpu.VMEM((4, 2, 2, rows // 4, head + LANES), bf16)
     lanes = (features // LANES, LANES)
     layer_scratch = [
         pltpu.VMEM((*grid, features // RANKS, head), bf16),
@@ -819,17 +825,15 @@
         message,
         pltpu.VMEM((RANKS, rows, LANES), bf16),
         dma((5,)),
-        dma((2, 3)),
-        dma((2, 3)),
+        *[dma((2, 3))] * 2,
         *[dma((2, 3, SIDE))] * 6,
         dma((3,)),
         dma((3,)),
-        *[dma((4, 2))] * 4,
+        *[dma((4, 2, 2))] * 4,
         *[dma((RANKS,))] * 3,
     ]
     wide_scratch = [
         pltpu.VMEM((8, quarter), f32),
-        pltpu.VMEM((features, columns), f32),
         pltpu.VMEM((2, 4, block, quarter), f32),
         pltpu.VMEM((2, block, quarter), f32),
         pltpu.VMEM((CHIPS, 2, 2, wide_half, quarter), bf16),
@@ -840,8 +844,8 @@
         pltpu.VMEM((tokens, LANES), f32),
         pltpu.VMEM((block, quarter), f32),
         pltpu.VMEM((3, 2 * SIDE, 8, quarter), f32),
-        dma((CHIPS, 2, 2)),
-        dma((CHIPS, 2, 2)),
+        dma((CHIPS, 2, 4)),
+        dma((CHIPS, 2, 4)),
         dma((CHIPS,)),
         dma((CHIPS,)),
         dma((CHIPS, 2)),
@@ -861,7 +865,7 @@
     return pl.pallas_call(
         functools.partial(kernel, 1e-5, 1.0 / math.sqrt(tokens), 0.5 / (tokens * columns * RANKS)),
         out_shape=(
-            jax.ShapeDtypeStruct((features, columns), bf16),
+            jax.ShapeDtypeStruct((features, columns), f32),
             jax.ShapeDtypeStruct((1, 1), f32),
         ),
         in_specs=[anywhere] * 7 + [smem],
@@ -893,7 +897,7 @@
         teacher_scales[None, :],
         perm,
     )
-    return (grad_proj, loss[0, 0])
+    return (grad_proj.astype(jnp.bfloat16), loss[0, 0])
 
 
 def solution(mesh):

time: 199 us -> 191 us (0.960)
  Pallas kernels: 194 us -> 185 us
  other arithmetic: 0 us -> 3.77 us
  local copies, waits for them, and re-layouts: 3.05 us -> 0 us
    pallas_call x1, Pallas kernels: 194 us -> 185 us  [distill(): pl.pallas_call(functools.partial(kernel, 1e-05, 1.0 / math.sqrt(tokens),...]
    convert_element_type x0 -> x1, other arithmetic: none -> 3.77 us  [shards(): return (grad_proj.astype(jnp.bfloat16), loss[0, 0])]
    unnamed x1 -> x0, local copies, waits for them, and re-layouts: 3.05 us -> none
where the time goes in v6:
time: 191 us
  Pallas kernels  185 us (97%)
  other arithmetic  3.77 us (2%)
  between operations  2.38 us (1%)
    pallas_call x1, Pallas kernels, distill(): pl.pallas_call(functools.partial(kernel, 1e-05, 1.0 / math.sqrt(tokens),...  185 us

profile of v6, /device:TPU:1, one launch (start us, length us, event | category | flops | bytes accessed | tf_op | source)
XLA Modules:
  0.0 190.8 jit_solution(3709684230601035785)
XLA Ops:
  0.6 184.6 %shard_map.95 = (f32[2048,512]{1,0:T(8,128)}, f32[1,1]{1,0:T(1,128)}) custom-call(bf16[128,2048]{1,0:T(8,128)(2,1)} %h_ref.1, bf16[4,4,4,2,64,512]{5,4,3,2,1,0:T(8,128)(2,1)} %bitcast.4, bf16[4,4,2,16,8192]{4,3,2,1,0:T(8,128)(2,1)} %bitcast.5, bf16[1,8192]{1,0:T(2,128)(2,1)} %gain_ref.1, bf16[2048,512]{1,0:T(8,128)(2,1)} %proj_ref.1, ...), custom_call_target="tpu_custom_call" | custom-call | tf_op jit(solution)/shard_map/pallas_call | solution.py:865
  185.3 3.8 %convert_element_type.3 = bf16[2048,512]{1,0:T(8,128)(2,1)} convert(f32[2048,512]{1,0:T(8,128)} %get-tuple-element.4) | non-fusion elementwise | flops 1048576 | bytes 6291456 | tf_op jit(solution)/shard_map/convert_element_type | solution.py:900

commit v7 on v6

--- a/solution.py
+++ b/solution.py
@@ -64,6 +64,8 @@
     near_recv,
     far_send,
     far_recv,
+    relay_send,
+    relay_recv,
     side_send,
     side_recv,
     gain_send,
@@ -160,6 +162,22 @@
             device_id_type=MESH,
         )
 
+    def relay_copy(kind, r, part, arrival):
+        place_of = spot[1 - kind]
+        at = lax.rem(place_of + (2 if arrival else 1 + 2 * part), SIDE)
+        there = lax.rem(place_of + 3 - 2 * part, SIDE)
+        pieces = pl.ds(2 * part, 2)
+        block = w_value.at[r, pieces, at, core] if kind == 0 else w_out.at[r, at, pieces, core]
+        chip = there * SIDE + y if kind == 1 else x * SIDE + there
+        return pltpu.make_async_remote_copy(
+            src_ref=block,
+            dst_ref=block,
+            send_sem=relay_send.at[kind, r - 1, part],
+            recv_sem=relay_recv.at[kind, r - 1, part],
+            device_id=(chip * 2 + core, z),
+            device_id_type=MESH,
+        )
+
     def side_copy(kind, r, j, owner):
         at = lax.rem(spot[1 - kind] + j, SIDE)
         block = w_value.at[r, :, at, owner] if kind == 0 else w_out.at[r, at, :, owner]
@@ -274,16 +292,32 @@
         for kind in range(2):
             for j in (1, 3, 2):
                 near_copy(kind, r, j, True).wait_recv()
-            for j in (1, 3, 2):
+            for j in (1, 3):
                 far_copy(kind, r, j, False).start()
         for kind in range(2):
             side_copy(kind, r, 0, core).start()
 
-    def settle(r, order):
-        for j in order:
+    def settle(k):
+        r = turn(k)
+        for part in range(2):
             for kind in range(2):
-                far_copy(kind, r, j, True).wait_recv()
+                far_copy(kind, r, 1 + 2 * part, True).wait_recv()
+                relay_copy(kind, r, part, False).start()
+
+        @pl.when(k < 2)
+        def _():
+            spread_far(k + 1)
+
+        for j in (1, 3):
+            for kind in range(2):
                 side_copy(kind, r, j, core).start()
+        for kind in range(2):
+            for part in range(2):
+                relay_copy(kind, r, part, True).wait_recv()
+            side_copy(kind, r, 2, core).start()
+        for kind in range(2):
+            for j in range(SIDE):
+                side_copy(kind, r, j, 1 - core).wait_recv()
 
     lax.fori_loop(0, 3, spread_near, 0)
     spread_far(0)
@@ -309,24 +343,9 @@
     def layer_step(layer, carry):
         r = lax.rem(layer - z + 4, 4)
 
-        @pl.when(layer != z)
-        def _():
-            settle(r, (1,))
-
-        @pl.when(layer < 2)
-        def _():
-            spread_far(layer + 1)
-
-        @pl.when(layer != z)
-        def _():
-            settle(r, (3, 2))
-            for kind in range(2):
-                for j in range(SIDE):
-                    side_copy(kind, r, j, 1 - core).wait_recv()
-
-        @pl.when(layer == 2)
-        def _():
-            lax.fori_loop(1, RANKS, send_codes, 0)
+        @pl.when(layer < z)
+        def _():
+            settle(layer)
 
         gain = gains[r].astype(jnp.float32)
         squares = jnp.zeros((rows, LANES), jnp.float32)
@@ -364,6 +383,15 @@
         order = [(k, part) for part in range(2) for k in range(2)]
         for k, part in order:
             leave(0, k, part)
+
+        @pl.when(jnp.logical_and(layer >= z, layer < 3))
+        def _():
+            settle(layer)
+
+        @pl.when(layer == 2)
+        def _():
+            lax.fori_loop(1, RANKS, send_codes, 0)
+
         for k, part in order:
             rows_in, so_far, squares = arrive(0, k, part)
             products[rows_in, :head] = so_far
@@ -395,8 +423,11 @@
                 first_copy(kind, j).wait_send()
                 for r in range(1, 4):
                     near_copy(kind, r, j, False).wait_send()
-                    far_copy(kind, r, j, False).wait_send()
+                    if j != 2:
+                        far_copy(kind, r, j, False).wait_send()
             for r in range(1, 4):
+                for part in range(2):
+                    relay_copy(kind, r, part, False).wait_send()
                 for j in range(SIDE):
                     side_copy(kind, r, j, core).wait_send()
         for layer in range(4):
@@ -738,7 +769,7 @@
     loss_ref[0, 0] = jnp.sum(squares[...]) * share
 
 
-LAYER_SCRATCH = 32
+LAYER_SCRATCH = 34
 
 
 def kernel(
@@ -826,7 +857,9 @@
         pltpu.VMEM((RANKS, rows, LANES), bf16),
         dma((5,)),
         *[dma((2, 3))] * 2,
-        *[dma((2, 3, SIDE))] * 6,
+        *[dma((2, 3, SIDE))] * 4,
+        *[dma((2, 3, 2))] * 2,
+        *[dma((2, 3, SIDE))] * 2,
         dma((3,)),
         dma((3,)),
         *[dma((4, 2, 2))] * 4,

time: 191 us -> 194 us (1.016)
  Pallas kernels: 185 us -> 187 us
    pallas_call x1, Pallas kernels: 185 us -> 187 us  [distill(): pl.pallas_call(functools.partial(kernel, 1e-05, 1.0 / math.sqrt(tokens),...]
where the time goes in v7:
time: 194 us; the launch traced here: 193 us
  Pallas kernels  187 us (96%)
  other arithmetic  3.77 us (2%)
  between operations  2.38 us (1%)
    pallas_call x1, Pallas kernels, distill(): pl.pallas_call(functools.partial(kernel, 1e-05, 1.0 / math.sqrt(tokens),...  187 us

profile of v7, /device:TPU:1, one launch (start us, length us, event | category | flops | bytes accessed | tf_op | source)
XLA Modules:
  0.0 193.3 jit_solution(5948116353150860781)
XLA Ops:
  0.6 187.2 %shard_map.95 = (f32[2048,512]{1,0:T(8,128)}, f32[1,1]{1,0:T(1,128)}) custom-call(bf16[128,2048]{1,0:T(8,128)(2,1)} %h_ref.1, bf16[4,4,4,2,64,512]{5,4,3,2,1,0:T(8,128)(2,1)} %bitcast.4, bf16[4,4,2,16,8192]{4,3,2,1,0:T(8,128)(2,1)} %bitcast.5, bf16[1,8192]{1,0:T(2,128)(2,1)} %gain_ref.1, bf16[2048,512]{1,0:T(8,128)(2,1)} %proj_ref.1, ...), custom_call_target="tpu_custom_call" | custom-call | tf_op jit(solution)/shard_map/pallas_call | solution.py:898
  187.8 3.8 %convert_element_type.3 = bf16[2048,512]{1,0:T(8,128)(2,1)} convert(f32[2048,512]{1,0:T(8,128)} %get-tuple-element.4) | non-fusion elementwise | flops 1048576 | bytes 6291456 | tf_op jit(solution)/shard_map/convert_element_type | solution.py:933

commit v8 on v6

--- a/solution.py
+++ b/solution.py
@@ -60,6 +60,7 @@
     own_sem,
     first_send,
     first_recv,
+    late_send,
     near_send,
     near_recv,
     far_send,
@@ -84,7 +85,7 @@
     rows, features = hidden_ref.shape
     head = value_ref.shape[-1]
     half = rows // 2
-    quarter = rows // 4
+    quarter = rows // 8
     weights = (w_value, w_out)
     width = 4 * features
 
@@ -159,6 +160,30 @@
             device_id=(chip * 2 + core, z),
             device_id_type=MESH,
         )
+
+    def late_copy(kind, j):
+        to = lax.rem(z + j, 4)
+        at = lax.rem(spot[1 - kind] + 2, SIDE)
+        if kind == 0:
+            source = value_ref.at[to, :, at, core]
+            target = w_value.at[4 - j, :, at, core]
+        else:
+            source = out_ref.at[at, :, core, :, pl.ds(pl.multiple_of(to * features, features), features)]
+            target = w_out.at[4 - j, at, :, core]
+        return pltpu.make_async_remote_copy(
+            src_ref=source,
+            dst_ref=target,
+            send_sem=late_send.at[kind, j - 1],
+            recv_sem=far_recv.at[kind, 3 - j, at],
+            device_id=(dp, to),
+            device_id_type=MESH,
+        )
+
+    def gives_late(j):
+        return jnp.logical_and(z >= 1, z < lax.rem(z + j, 4))
+
+    def takes_late(k):
+        return jnp.logical_and(k >= 1, k < z)
 
     def side_copy(kind, r, j, owner):
         at = lax.rem(spot[1 - kind] + j, SIDE)
@@ -240,6 +265,13 @@
     for j in (1, 3, 2):
         first_copy(0, j).start()
         first_copy(1, j).start()
+    for j in (1, 2):
+
+        @pl.when(gives_late(j))
+        def _():
+            for kind in range(2):
+                late_copy(kind, j).start()
+
     for copy in own_copies():
         copy.start()
 
@@ -274,8 +306,13 @@
         for kind in range(2):
             for j in (1, 3, 2):
                 near_copy(kind, r, j, True).wait_recv()
-            for j in (1, 3, 2):
+            for j in (1, 3):
                 far_copy(kind, r, j, False).start()
+
+            @pl.when(jnp.logical_not(takes_late(k)))
+            def _():
+                far_copy(kind, r, 2, False).start()
+
         for kind in range(2):
             side_copy(kind, r, 0, core).start()
 
@@ -361,7 +398,7 @@
             so_far = products[rows_in, :head] + buffer[layer, k, part, :, :head].astype(jnp.float32)
             return rows_in, so_far, products[rows_in, head:] + marks + pltpu.roll(marks, LANES // 2, 1)
 
-        order = [(k, part) for part in range(2) for k in range(2)]
+        order = [(k, part) for part in range(4) for k in range(2)]
         for k, part in order:
             leave(0, k, part)
         for k, part in order:
@@ -395,13 +432,26 @@
                 first_copy(kind, j).wait_send()
                 for r in range(1, 4):
                     near_copy(kind, r, j, False).wait_send()
-                    far_copy(kind, r, j, False).wait_send()
+                    if j != 2:
+                        far_copy(kind, r, j, False).wait_send()
+            for j in (1, 2):
+
+                @pl.when(gives_late(j))
+                def _():
+                    late_copy(kind, j).wait_send()
+
+            for k in range(3):
+
+                @pl.when(jnp.logical_not(takes_late(k)))
+                def _():
+                    far_copy(kind, turn(k), 2, False).wait_send()
+
             for r in range(1, 4):
                 for j in range(SIDE):
                     side_copy(kind, r, j, core).wait_send()
         for layer in range(4):
             for k in range(2):
-                for part in range(2):
+                for part in range(4):
                     for phase in range(2):
                         sum_copy(phase, layer, k, part).wait_send()
 
@@ -431,10 +481,13 @@
     store_ref,
     perm_ref,
     proj_ref,
-    total,
+    grad_ref,
     loss_ref,
     held,
     squares,
+    total,
+    rounded,
+    rounded_sem,
     y_own,
     y_keep,
     out1,
@@ -731,14 +784,23 @@
 
     lax.fori_loop(0, steps + 6, body, 0)
 
+    def piece_out(f):
+        rows = pl.ds(f * 256, 256)
+        return pltpu.make_async_copy(rounded.at[rows], grad_ref.at[rows], rounded_sem.at[f])
+
+    for f in range(8):
+        rounded[f * 256 : (f + 1) * 256, :] = total[f * 256 : (f + 1) * 256, :].astype(jnp.bfloat16)
+        piece_out(f).start()
     loss_in(2)
     for group in range(3):
         for j in range(1, sizes[group]):
             loss_copy(group, j, False).wait_send()
     loss_ref[0, 0] = jnp.sum(squares[...]) * share
-
-
-LAYER_SCRATCH = 32
+    for f in range(8):
+        piece_out(f).wait()
+
+
+LAYER_SCRATCH = 33
 
 
 def kernel(
@@ -807,7 +869,7 @@
     folded_out = folded_out.reshape(*grid[1:], head // RANKS, 4 * features)
     bf16, f32 = jnp.bfloat16, jnp.float32
     dma = pltpu.SemaphoreType.DMA
-    message = pltpu.VMEM((4, 2, 2, rows // 4, head + LANES), bf16)
+    message = pltpu.VMEM((4, 2, 4, rows // 8, head + LANES), bf16)
     lanes = (features // LANES, LANES)
     layer_scratch = [
         pltpu.VMEM((*grid, features // RANKS, head), bf16),
@@ -825,15 +887,18 @@
         message,
         pltpu.VMEM((RANKS, rows, LANES), bf16),
         dma((5,)),
-        *[dma((2, 3))] * 2,
+        *[dma((2, 3))] * 3,
         *[dma((2, 3, SIDE))] * 6,
         dma((3,)),
         dma((3,)),
-        *[dma((4, 2, 2))] * 4,
+        *[dma((4, 2, 4))] * 4,
         *[dma((RANKS,))] * 3,
     ]
     wide_scratch = [
         pltpu.VMEM((8, quarter), f32),
+        pltpu.VMEM((features, columns), f32),
+        pltpu.VMEM((features, columns), bf16),
+        dma((8,)),
         pltpu.VMEM((2, 4, block, quarter), f32),
         pltpu.VMEM((2, block, quarter), f32),
         pltpu.VMEM((CHIPS, 2, 2, wide_half, quarter), bf16),
@@ -859,17 +924,16 @@
         dma((3, 2 * SIDE)),
         dma((3, 2 * SIDE)),
     ]
-    vmem = pl.BlockSpec(memory_space=pltpu.VMEM)
     smem = pl.BlockSpec(memory_space=pltpu.SMEM)
     anywhere = pl.BlockSpec(memory_space=pl.ANY)
     return pl.pallas_call(
         functools.partial(kernel, 1e-5, 1.0 / math.sqrt(tokens), 0.5 / (tokens * columns * RANKS)),
         out_shape=(
-            jax.ShapeDtypeStruct((features, columns), f32),
+            jax.ShapeDtypeStruct((features, columns), bf16),
             jax.ShapeDtypeStruct((1, 1), f32),
         ),
         in_specs=[anywhere] * 7 + [smem],
-        out_specs=(vmem, smem),
+        out_specs=(anywhere, smem),
         scratch_shapes=[
             pltpu.VMEM((CHIPS, block, features), bf16),
             pltpu.VMEM((tokens, LANES), bf16),
@@ -897,7 +961,7 @@
         teacher_scales[None, :],
         perm,
     )
-    return (grad_proj.astype(jnp.bfloat16), loss[0, 0])
+    return (grad_proj, loss[0, 0])
 
 
 def solution(mesh):

time: 191 us -> 189 us (0.990)
  other arithmetic: 3.77 us -> 0 us
  local copies, waits for them, and re-layouts: 0 us -> 3.05 us
    convert_element_type x1 -> x0, other arithmetic: 3.77 us -> none  [shards(): return (grad_proj.astype(jnp.bfloat16), loss[0, 0])]
    unnamed x0 -> x1, local copies, waits for them, and re-layouts: none -> 3.05 us
where the time goes in v8:
time: 189 us
  Pallas kernels  184 us (97%)
  local copies, waits for them, and re-layouts  3.05 us (2%)
  between operations  2.38 us (1%)
    pallas_call x1, Pallas kernels, distill(): pl.pallas_call(functools.partial(kernel, 1e-05, 1.0 / math.sqrt(tokens),...  184 us

profile of v8, /device:TPU:1, one launch (start us, length us, event | category | flops | bytes accessed | tf_op | source)
XLA Modules:
  0.0 188.9 jit_solution(669504989796335591)
XLA Ops:
  0.6 183.5 %shard_map.95 = (bf16[2048,512]{1,0:T(8,128)(2,1)}, f32[1,1]{1,0:T(1,128)}) custom-call(bf16[128,2048]{1,0:T(8,128)(2,1)} %h_ref.1, bf16[4,4,4,2,64,512]{5,4,3,2,1,0:T(8,128)(2,1)} %bitcast.4, bf16[4,4,2,16,8192]{4,3,2,1,0:T(8,128)(2,1)} %bitcast.5, bf16[1,8192]{1,0:T(2,128)(2,1)} %gain_ref.1, bf16[2048,512]{1,0:T(8,128)(2,1)} %proj_ref.1, ...), custom_call_target="tpu_custom_call" | custom-call | tf_op jit(solution)/shard_map/pallas_call | solution.py:929
  184.1 3.0 %copy.12 = bf16[2048,512]{1,0:T(8,128)(2,1)} copy(bf16[2048,512]{1,0:T(8,128)(2,1)} %get-tuple-element.8) | data formatting | bytes 4194304

commit v9 on v8

--- a/solution.py
+++ b/solution.py
@@ -323,7 +323,11 @@
                 side_copy(kind, r, j, core).start()
 
     lax.fori_loop(0, 3, spread_near, 0)
-    spread_far(0)
+    def spread_all(k, carry):
+        spread_far(k)
+        return carry
+
+    lax.fori_loop(0, 3, spread_all, 0)
     scale = jnp.broadcast_to(scale_row[...].astype(jnp.float32), (rows, LANES)).T
 
     def scale_codes(d, carry):
@@ -348,15 +352,7 @@
 
         @pl.when(layer != z)
         def _():
-            settle(r, (1,))
-
-        @pl.when(layer < 2)
-        def _():
-            spread_far(layer + 1)
-
-        @pl.when(layer != z)
-        def _():
-            settle(r, (3, 2))
+            settle(r, (1, 3, 2))
             for kind in range(2):
                 for j in range(SIDE):
                     side_copy(kind, r, j, 1 - core).wait_recv()

time: 189 us -> 189 us (level)
  no operation moved by 1% of the time
where the time goes in v9:
time: 189 us; the launch traced here: 188 us
  Pallas kernels  183 us (97%)
  local copies, waits for them, and re-layouts  3.05 us (2%)
  between operations  2.38 us (1%)
    pallas_call x1, Pallas kernels, distill(): pl.pallas_call(functools.partial(kernel, 1e-05, 1.0 / math.sqrt(tokens),...  183 us

profile of v9, /device:TPU:1, one launch (start us, length us, event | category | flops | bytes accessed | tf_op | source)
XLA Modules:
  0.0 188.3 jit_solution(3653613169520273339)
XLA Ops:
  0.6 182.9 %shard_map.95 = (bf16[2048,512]{1,0:T(8,128)(2,1)}, f32[1,1]{1,0:T(1,128)}) custom-call(bf16[128,2048]{1,0:T(8,128)(2,1)} %h_ref.1, bf16[4,4,4,2,64,512]{5,4,3,2,1,0:T(8,128)(2,1)} %bitcast.4, bf16[4,4,2,16,8192]{4,3,2,1,0:T(8,128)(2,1)} %bitcast.5, bf16[1,8192]{1,0:T(2,128)(2,1)} %gain_ref.1, bf16[2048,512]{1,0:T(8,128)(2,1)} %proj_ref.1, ...), custom_call_target="tpu_custom_call" | custom-call | tf_op jit(solution)/shard_map/pallas_call | solution.py:925
  183.5 3.0 %copy.12 = bf16[2048,512]{1,0:T(8,128)(2,1)} copy(bf16[2048,512]{1,0:T(8,128)(2,1)} %get-tuple-element.8) | data formatting | bytes 4194304

commit v10 on v9

--- a/solution.py
+++ b/solution.py
@@ -316,8 +316,9 @@
         for kind in range(2):
             side_copy(kind, r, 0, core).start()
 
-    def settle(r, order):
-        for j in order:
+    def serve(k):
+        r = turn(k)
+        for j in (1, 3, 2):
             for kind in range(2):
                 far_copy(kind, r, j, True).wait_recv()
                 side_copy(kind, r, j, core).start()
@@ -328,6 +329,7 @@
         return carry
 
     lax.fori_loop(0, 3, spread_all, 0)
+
     scale = jnp.broadcast_to(scale_row[...].astype(jnp.float32), (rows, LANES)).T
 
     def scale_codes(d, carry):
@@ -352,14 +354,9 @@
 
         @pl.when(layer != z)
         def _():
-            settle(r, (1, 3, 2))
             for kind in range(2):
                 for j in range(SIDE):
                     side_copy(kind, r, j, 1 - core).wait_recv()
-
-        @pl.when(layer == 2)
-        def _():
-            lax.fori_loop(1, RANKS, send_codes, 0)
 
         gain = gains[r].astype(jnp.float32)
         squares = jnp.zeros((rows, LANES), jnp.float32)
@@ -402,6 +399,19 @@
             products[rows_in, :head] = so_far
             products[rows_in, head:] = squares
             leave(1, k, part)
+
+        @pl.when(layer + 1 < z)
+        def _():
+            serve(layer + 1)
+
+        @pl.when(jnp.logical_and(layer >= z, layer < 3))
+        def _():
+            serve(layer)
+
+        @pl.when(layer == 2)
+        def _():
+            lax.fori_loop(1, RANKS, send_codes, 0)
+
         for k, part in order:
             rows_in, so_far, squares = arrive(1, k, part)
             scale = lax.rsqrt(squares * (1.0 / width) + eps)
@@ -419,6 +429,10 @@
                 jnp.bfloat16
             )
         return carry
+
+    @pl.when(z > 0)
+    def _():
+        serve(0)
 
     lax.fori_loop(0, 4, layer_step, 0)
 

time: 189 us -> 180 us (0.952)
  Pallas kernels: 183 us -> 174 us
    pallas_call x1, Pallas kernels: 183 us -> 174 us  [distill(): pl.pallas_call(functools.partial(kernel, 1e-05, 1.0 / math.sqrt(tokens),...]
where the time goes in v10:
time: 180 us
  Pallas kernels  174 us (97%)
  local copies, waits for them, and re-layouts  3.05 us (2%)
  between operations  2.38 us (1%)
    pallas_call x1, Pallas kernels, distill(): pl.pallas_call(functools.partial(kernel, 1e-05, 1.0 / math.sqrt(tokens),...  174 us

profile of v10, /device:TPU:1, one launch (start us, length us, event | category | flops | bytes accessed | tf_op | source)
XLA Modules:
  0.0 179.8 jit_solution(6220945002491660539)
XLA Ops:
  0.6 174.4 %shard_map.95 = (bf16[2048,512]{1,0:T(8,128)(2,1)}, f32[1,1]{1,0:T(1,128)}) custom-call(bf16[128,2048]{1,0:T(8,128)(2,1)} %h_ref.1, bf16[4,4,4,2,64,512]{5,4,3,2,1,0:T(8,128)(2,1)} %bitcast.4, bf16[4,4,2,16,8192]{4,3,2,1,0:T(8,128)(2,1)} %bitcast.5, bf16[1,8192]{1,0:T(2,128)(2,1)} %gain_ref.1, bf16[2048,512]{1,0:T(8,128)(2,1)} %proj_ref.1, ...), custom_call_target="tpu_custom_call" | custom-call | tf_op jit(solution)/shard_map/pallas_call | solution.py:939
  175.1 3.0 %copy.12 = bf16[2048,512]{1,0:T(8,128)(2,1)} copy(bf16[2048,512]{1,0:T(8,128)(2,1)} %get-tuple-element.8) | data formatting | bytes 4194304

commit v11 on v10

--- a/solution.py
+++ b/solution.py
@@ -394,6 +394,11 @@
         order = [(k, part) for part in range(4) for k in range(2)]
         for k, part in order:
             leave(0, k, part)
+
+        @pl.when(layer == 2)
+        def _():
+            lax.fori_loop(1, CHIPS, send_codes, 0)
+
         for k, part in order:
             rows_in, so_far, squares = arrive(0, k, part)
             products[rows_in, :head] = so_far
@@ -410,7 +415,7 @@
 
         @pl.when(layer == 2)
         def _():
-            lax.fori_loop(1, RANKS, send_codes, 0)
+            lax.fori_loop(CHIPS, RANKS, send_codes, 0)
 
         for k, part in order:
             rows_in, so_far, squares = arrive(1, k, part)

time: 180 us -> 180 us (level)
  no operation moved by 1% of the time
where the time goes in v11:
time: 180 us
  Pallas kernels  174 us (97%)
  local copies, waits for them, and re-layouts  3.05 us (2%)
  between operations  2.38 us (1%)
    pallas_call x1, Pallas kernels, distill(): pl.pallas_call(functools.partial(kernel, 1e-05, 1.0 / math.sqrt(tokens),...  174 us

profile of v11, /device:TPU:1, one launch (start us, length us, event | category | flops | bytes accessed | tf_op | source)
XLA Modules:
  0.0 179.6 jit_solution(2302632655667875333)
XLA Ops:
  0.6 174.2 %shard_map.95 = (bf16[2048,512]{1,0:T(8,128)(2,1)}, f32[1,1]{1,0:T(1,128)}) custom-call(bf16[128,2048]{1,0:T(8,128)(2,1)} %h_ref.1, bf16[4,4,4,2,64,512]{5,4,3,2,1,0:T(8,128)(2,1)} %bitcast.4, bf16[4,4,2,16,8192]{4,3,2,1,0:T(8,128)(2,1)} %bitcast.5, bf16[1,8192]{1,0:T(2,128)(2,1)} %gain_ref.1, bf16[2048,512]{1,0:T(8,128)(2,1)} %proj_ref.1, ...), custom_call_target="tpu_custom_call" | custom-call | tf_op jit(solution)/shard_map/pallas_call | solution.py:944
  174.8 3.0 %copy.12 = bf16[2048,512]{1,0:T(8,128)(2,1)} copy(bf16[2048,512]{1,0:T(8,128)(2,1)} %get-tuple-element.8) | data formatting | bytes 4194304
